TPU v7x, 128 devices: a whole 4x4x4 slice. The times are simulated.
128 devices in a mesh: dp: 2 (over core), seq: 16 (over x, z), head: 4 (over y).
Axes of the slice: x: 4, y: 4, z: 4, core: 2. Of those that a mesh axis runs over, the one named last changes fastest.
Arguments:
- hidden: bfloat16 [2, 8192, 1536], P('dp', 'seq'), may hold values from -6 to 6
- cotangent: bfloat16 [2, 8192, 1536], P('dp', 'seq'), may hold values from -6 to 6
- norm_gain: float32 [1536], replicated, may hold values from 0.1 to 1.9
- w_z: bfloat16 [1536, 3072], P(None, 'head'), may hold values from -0.15625 to 0.15625
- w_x: bfloat16 [1536, 3072], P(None, 'head'), may hold values from -0.15625 to 0.15625
- w_bc: bfloat16 [1536, 256], replicated, may hold values from -0.15625 to 0.15625
- w_dt: bfloat16 [1536, 48], P(None, 'head'), may hold values from -0.3125 to 0.3125
- conv_x: float32 [4, 3072], P(None, 'head'), may hold values from -3 to 3
- conv_bc: float32 [4, 256], replicated, may hold values from -3 to 3
- bias_x: float32 [3072], P('head'), may hold values from -3 to 3
- bias_bc: float32 [256], replicated, may hold values from -3 to 3
- dt_bias: float32 [48], P('head'), may hold values from -6.5 to -4.5
- a_log: float32 [48], P('head'), may hold values from -4.6 to 0.7
- skip_d: float32 [48], P('head'), may hold values from 0.5 to 1.5
- gain_out: float32 [3072], P('head'), may hold values from 0.1 to 1.9
- w_out: bfloat16 [3072, 1536], P('head'), may hold values from -0.109375 to 0.109375
Outputs:
- output: bfloat16 [2, 8192, 1536], P('dp', 'seq', 'head')
- hidden_grad: bfloat16 [2, 8192, 1536], P('dp', 'seq', 'head')
- grad_norm_gain: float32 [1536], P('head')
- grad_w_z: float32 [1536, 3072], P(None, 'head')
- grad_w_x: float32 [1536, 3072], P(None, 'head')
- grad_w_bc: float32 [1536, 256], P(None, 'head')
- grad_w_dt: float32 [1536, 48], P(None, 'head')
- grad_conv_x: float32 [4, 3072], P(None, 'head')
- grad_conv_bc: float32 [4, 256], replicated
- grad_bias_x: float32 [3072], P('head')
- grad_bias_bc: float32 [256], replicated
- grad_dt_bias: float32 [48], P('head')
- grad_a_log: float32 [48], P('head')
- grad_skip_d: float32 [48], P('head')
- grad_gain_out: float32 [3072], P('head')
- grad_w_out: float32 [3072, 1536], P('head')
All inputs are finite; a program needn't handle non-finite values.
Results may differ from a plain program's by a relative error of at most 0.012.
The roundings to bfloat16 on the way count: a program that leaves them out, or rounds other values in their place, can miss the bound.
Values sent between devices are 32-bit elements; how exact they have to be, the bound alone decides.
No kernel may reach another device: no remote copies, remote signals or barrier semaphores. Data moves between devices by JAX's collectives and lax.ppermute only.
A program may use at most 192 MiB of HBM per device.

v0:
```python
import jax
import jax.numpy as jnp
from jax import lax
from jax.sharding import PartitionSpec as P

HEADDIM = 64
STATE = 128
SPAN = 256


epsilon = 1e-05
highest = lax.Precision.HIGHEST


def from_behind(shard, axis, by):
    peers = lax.axis_size(axis)
    pairs = [(i, i + by) for i in range(peers) if 0 <= i + by < peers]
    return lax.ppermute(shard, axis, pairs)


def rounded(value):
    return lax.optimization_barrier(value.astype(jnp.bfloat16)).astype(jnp.float32)


def silu_slope(value):
    sigma_value = jax.nn.sigmoid(value)
    return sigma_value * (1.0 + value * (1.0 - sigma_value))


def causal_conv(edge_rows, rows_now, kernel, bias_row):
    extended = jnp.concatenate([edge_rows, rows_now], axis=0)
    taps_count = kernel.shape[0]
    row_count = rows_now.shape[0]
    summed = jnp.zeros(rows_now.shape, jnp.float32) + bias_row[None, :]
    for offset in range(taps_count):
        summed = summed + kernel[offset][None, :] * extended[offset : offset + row_count]
    return (summed, extended)


def conv_back(grad_rows, extended, kernel):
    taps_count = kernel.shape[0]
    row_count = grad_rows.shape[0]
    grad_ext = jnp.zeros(extended.shape, jnp.float32)
    kernel_rows = []
    for offset in range(taps_count):
        grad_ext = grad_ext + jnp.pad(
            kernel[offset][None, :] * grad_rows, ((offset, taps_count - 1 - offset), (0, 0))
        )
        kernel_rows.append(jnp.sum(grad_rows * extended[offset : offset + row_count], axis=0))
    return (grad_ext, jnp.stack(kernel_rows, axis=0), jnp.sum(grad_rows, axis=0))


def block_step(carry_state, block_data):
    values, keys_b, reads_c, step_size, log_decay = block_data
    cumulated = jnp.cumsum(log_decay, axis=0)
    positions = jnp.arange(log_decay.shape[0])
    causal = (positions[:, None] >= positions[None, :])[None]
    scores = jnp.dot(reads_c, keys_b.T, precision=highest)
    spread_cum = cumulated.T[:, :, None] - cumulated.T[:, None, :]
    decayed = jnp.where(causal, jnp.exp(jnp.where(causal, spread_cum, 0.0)), 0.0)
    mixing = decayed * scores[None] * step_size.T[:, None, :]
    within = jnp.einsum("hts,shp->thp", mixing, values, precision=highest)
    carried = (
        jnp.einsum("tn,hpn->thp", reads_c, carry_state, precision=highest)
        * jnp.exp(cumulated)[:, :, None]
    )
    last_cum = cumulated[-1]
    weights = jnp.exp(last_cum[None, :] - cumulated) * step_size
    next_state = jnp.exp(last_cum)[:, None, None] * carry_state + jnp.einsum(
        "sh,shp,sn->hpn", weights, values, keys_b, precision=highest
    )
    return (next_state, within + carried)


def ssd_outputs(values, keys_b, reads_c, step_size, log_decay, start_state):
    length = values.shape[0]
    blocks = length // SPAN

    def split_rows(member):
        return member.reshape((blocks, SPAN) + member.shape[1:])

    final_state, outputs = lax.scan(
        jax.checkpoint(block_step),
        start_state,
        (
            split_rows(values),
            split_rows(keys_b),
            split_rows(reads_c),
            split_rows(step_size),
            split_rows(log_decay),
        ),
    )
    return outputs.reshape(values.shape)


def device_state(values, keys_b, step_size, log_decay, start_state):
    cumulated = jnp.cumsum(log_decay, axis=0)
    last_cum = cumulated[-1]
    weights = jnp.exp(last_cum[None, :] - cumulated) * step_size
    return jnp.exp(last_cum)[:, None, None] * start_state + jnp.einsum(
        "sh,shp,sn->hpn", weights, values, keys_b, precision=highest
    )


def per_device(
    hidden,
    cotangent,
    norm_gain,
    w_z,
    w_x,
    w_bc,
    w_dt,
    conv_x,
    conv_bc,
    bias_x,
    bias_bc,
    dt_bias,
    a_log,
    skip_d,
    gain_out,
    w_out,
):
    rows_in = hidden[0].astype(jnp.float32)
    tokens = rows_in.shape[0]
    model_width = rows_in.shape[1]
    heads_here = w_dt.shape[1]
    inner_here = w_z.shape[1]
    parts_head = lax.axis_size("head")
    head_pos = lax.axis_index("head")
    share_width = model_width // parts_head
    share_start = head_pos * share_width
    bc_share = w_bc.shape[1] // parts_head
    edge_count = conv_x.shape[0] - 1
    scale_in = lax.rsqrt(jnp.mean(rows_in * rows_in, axis=1, keepdims=True) + epsilon)
    unit_rows = rows_in * scale_in
    normed = (unit_rows * norm_gain).astype(jnp.bfloat16)
    gate_z = jnp.dot(normed, w_z, preferred_element_type=jnp.float32)
    inner_x = jnp.dot(normed, w_x, preferred_element_type=jnp.float32)
    inner_bc = jnp.dot(normed, w_bc, preferred_element_type=jnp.float32)
    step_raw = jnp.dot(normed, w_dt, preferred_element_type=jnp.float32)
    edge_rows = jnp.concatenate(
        [inner_x[tokens - edge_count :], inner_bc[tokens - edge_count :]], axis=1
    )
    edge_prev = from_behind(edge_rows, "seq", 1)
    pre_x, ext_x = causal_conv(edge_prev[:, :inner_here], inner_x, conv_x, bias_x)
    pre_bc, ext_bc = causal_conv(edge_prev[:, inner_here:], inner_bc, conv_bc, bias_bc)
    act_x = jax.nn.silu(pre_x)
    act_bc = jax.nn.silu(pre_bc)
    values = rounded(act_x).reshape(tokens, heads_here, HEADDIM)
    bc_low = rounded(act_bc)
    keys_b = bc_low[:, :STATE]
    reads_c = bc_low[:, STATE:]
    step_input = step_raw + dt_bias[None, :]
    step_size = jax.nn.softplus(step_input)
    decay_rate = jnp.exp(a_log)[None, :]
    log_decay = -decay_rate * step_size
    decay_here = jnp.exp(jnp.sum(log_decay, axis=0))
    empty_state = jnp.zeros((heads_here, HEADDIM, STATE), jnp.float32)
    local_state = device_state(values, keys_b, step_size, log_decay, empty_state)

    def forward_turn(turn_index, received):
        return from_behind(decay_here[:, None, None] * received + local_state, "seq", 1)

    incoming = lax.fori_loop(0, lax.axis_size("seq") - 1, forward_turn, empty_state)
    ssd_rows, ssd_pull = jax.vjp(
        ssd_outputs, values, keys_b, reads_c, step_size, log_decay, incoming
    )
    skip_cols = jnp.repeat(skip_d, HEADDIM)[None, :]
    mixed_out = ssd_rows.reshape(tokens, inner_here) + skip_cols * act_x
    silu_z = jax.nn.silu(gate_z)
    gated_out = mixed_out * silu_z
    inner_all = inner_here * parts_head
    square_total = lax.psum(jnp.sum(gated_out * gated_out, axis=1), "head")
    scale_out = lax.rsqrt(square_total / inner_all + epsilon)[:, None]
    unit_out = gated_out * scale_out
    normed_out = (unit_out * gain_out).astype(jnp.bfloat16)
    branch_terms = jnp.dot(normed_out, w_out, preferred_element_type=jnp.float32)
    branch_own = lax.psum_scatter(branch_terms, "head", scatter_dimension=1, tiled=True)
    rows_own = lax.dynamic_slice_in_dim(rows_in, share_start, share_width, 1)
    output = (rows_own + branch_own).astype(jnp.bfloat16)[None]
    cot_rows = cotangent[0]
    grad_w_out = jnp.einsum("ti,td->id", normed_out, cot_rows, preferred_element_type=jnp.float32)
    grad_normed_out = jnp.einsum("td,id->ti", cot_rows, w_out, preferred_element_type=jnp.float32)
    grad_gain_out = jnp.sum(grad_normed_out * unit_out, axis=0)
    grad_unit_out = grad_normed_out * gain_out
    dot_total = lax.psum(jnp.sum(grad_unit_out * unit_out, axis=1), "head")
    grad_gated = scale_out * (grad_unit_out - unit_out * (dot_total / inner_all)[:, None])
    grad_mixed = rounded(grad_gated * silu_z)
    grad_gate = (grad_gated * mixed_out * silu_slope(gate_z)).astype(jnp.bfloat16)
    grad_skip_d = jnp.sum((grad_mixed * act_x).reshape(tokens, heads_here, HEADDIM), axis=(0, 2))
    grads_local = ssd_pull(grad_mixed.reshape(tokens, heads_here, HEADDIM))
    own_back = grads_local[5]

    def backward_turn(turn_index, received):
        return from_behind(decay_here[:, None, None] * received + own_back, "seq", -1)

    later_grad = lax.fori_loop(0, lax.axis_size("seq") - 1, backward_turn, empty_state)
    unused_end, state_pull = jax.vjp(device_state, values, keys_b, step_size, log_decay, incoming)
    grads_state = state_pull(later_grad)
    grad_values = grads_local[0] + grads_state[0]
    grad_keys = grads_local[1] + grads_state[1]
    grad_reads = grads_local[2]
    grad_log = grads_local[4] + grads_state[3]
    grad_step = grads_local[3] + grads_state[2] - decay_rate * grad_log
    grad_a_log = jnp.sum(grad_log * log_decay, axis=0)
    grad_step_pre = grad_step * jax.nn.sigmoid(step_input)
    grad_dt_bias = jnp.sum(grad_step_pre, axis=0)
    grad_step_low = grad_step_pre.astype(jnp.bfloat16)
    grad_act_x = grad_values.reshape(tokens, inner_here) + grad_mixed * skip_cols
    grad_act_bc = lax.psum(jnp.concatenate([grad_keys, grad_reads], axis=1), "head")
    grad_ext_x, grad_conv_x, grad_bias_x = conv_back(grad_act_x * silu_slope(pre_x), ext_x, conv_x)
    grad_ext_bc, grad_conv_bc, grad_bias_bc = conv_back(
        grad_act_bc * silu_slope(pre_bc), ext_bc, conv_bc
    )
    edge_grads = jnp.concatenate([grad_ext_x[:edge_count], grad_ext_bc[:edge_count]], axis=1)
    edge_next = from_behind(edge_grads, "seq", -1)
    tail_pad = ((tokens - edge_count, 0), (0, 0))
    grad_x_low = (grad_ext_x[edge_count:] + jnp.pad(edge_next[:, :inner_here], tail_pad)).astype(
        jnp.bfloat16
    )
    grad_bc_low = (grad_ext_bc[edge_count:] + jnp.pad(edge_next[:, inner_here:], tail_pad)).astype(
        jnp.bfloat16
    )
    grad_bc_share = lax.dynamic_slice_in_dim(grad_bc_low, head_pos * bc_share, bc_share, 1)
    w_bc_share = lax.dynamic_slice_in_dim(w_bc, head_pos * bc_share, bc_share, 1)
    grad_w_z = jnp.einsum("td,ti->di", normed, grad_gate, preferred_element_type=jnp.float32)
    grad_w_x = jnp.einsum("td,ti->di", normed, grad_x_low, preferred_element_type=jnp.float32)
    grad_w_bc = jnp.einsum("td,ti->di", normed, grad_bc_share, preferred_element_type=jnp.float32)
    grad_w_dt = jnp.einsum("td,ti->di", normed, grad_step_low, preferred_element_type=jnp.float32)
    grad_normed = jnp.einsum("ti,di->td", grad_gate, w_z, preferred_element_type=jnp.float32)
    grad_normed = grad_normed + jnp.einsum(
        "ti,di->td", grad_x_low, w_x, preferred_element_type=jnp.float32
    )
    grad_normed = grad_normed + jnp.einsum(
        "ti,di->td", grad_bc_share, w_bc_share, preferred_element_type=jnp.float32
    )
    grad_normed = grad_normed + jnp.einsum(
        "ti,di->td", grad_step_low, w_dt, preferred_element_type=jnp.float32
    )
    grad_norm_own = lax.psum_scatter(grad_normed, "head", scatter_dimension=1, tiled=True)
    unit_own = lax.dynamic_slice_in_dim(unit_rows, share_start, share_width, 1)
    scale_gain = lax.dynamic_slice_in_dim(norm_gain, share_start, share_width, 0)
    grad_norm_gain = jnp.sum(grad_norm_own * unit_own, axis=0)
    grad_unit_in = grad_norm_own * scale_gain
    row_dot = lax.psum(jnp.sum(grad_unit_in * unit_own, axis=1), "head")[:, None]
    grad_in = scale_in * (grad_unit_in - unit_own * row_dot / model_width)
    cot_own = lax.dynamic_slice_in_dim(cot_rows, share_start, share_width, 1).astype(jnp.float32)
    hidden_grad = (grad_in + cot_own).astype(jnp.bfloat16)[None]
    summed = lax.psum(
        (
            grad_norm_gain,
            grad_w_z,
            grad_w_x,
            grad_w_bc,
            grad_w_dt,
            grad_conv_x,
            grad_conv_bc,
            grad_bias_x,
            grad_bias_bc,
            grad_dt_bias,
            grad_a_log,
            grad_skip_d,
            grad_gain_out,
            grad_w_out,
        ),
        ("dp", "seq"),
    )
    return (
        output,
        hidden_grad,
        summed[0],
        summed[1],
        summed[2],
        summed[3],
        summed[4],
        summed[5],
        summed[6],
        summed[7],
        summed[8],
        summed[9],
        summed[10],
        summed[11],
        summed[12],
        summed[13],
    )


def solution(mesh):
    placed = (
        P("dp", "seq", None),
        P("dp", "seq", None),
        P(),
        P(None, "head"),
        P(None, "head"),
        P(),
        P(None, "head"),
        P(None, "head"),
        P(),
        P("head"),
        P(),
        P("head"),
        P("head"),
        P("head"),
        P("head"),
        P("head", None),
    )
    return jax.shard_map(
        per_device,
        mesh=mesh,
        in_specs=placed,
        out_specs=(
            P("dp", "seq", "head"),
            P("dp", "seq", "head"),
            P("head"),
            P(None, "head"),
            P(None, "head"),
            P(None, "head"),
            P(None, "head"),
            P(None, "head"),
            P(),
            P("head"),
            P(),
            P("head"),
            P("head"),
            P("head"),
            P("head"),
            P("head", None),
        ),
        check_vma=False,
    )
```

profile of v0, /device:TPU:1, one launch (start us, length us, event | category | flops | bytes accessed | tf_op | source)
XLA Modules:
  0.0 1074.5 jit_solution(14530894452559257299)
XLA Ops:
  39.3 187.8 %while.63 = (s32[]{:T(128)}, f32[12,64,128]{2,1,0:T(8,128)S(1)}, f32[12]{0:T(128)S(1)}, f32[12,64,128]{2,1,0:T(8,128)S(1)}, s32[]{:T(128)}) while((s32[]{:T(128)}, f32[12,64,128]{2,1,0:T(8,128)S(1)}, f32[12]{0:T(128)S(1)}, f32[12,64,128]{2,1,0:T(8,128)S(1)}, s32[]{:T(128)}) %tuple.185), condition=%wide.region_5.6_spmd, body=%wide.region_4.5_spmd.sunk | while | flops 196610 | bytes 2752661 | solution.py:164
  234.9 59.3 %while.65 = (s32[]{:T(128)}, f32[12,64,128]{2,1,0:T(8,128)S(1)}, f32[2,256,12,64]{1,0,3,2:T(2,128)}, f32[2,12,64,128]{3,2,1,0:T(8,128)}, f32[2,256,12]{1,2,0:T(8...) while((s32[]{:T(128)}, f32[12,64,128]{2,1,0:T(8,128)S(1)}, ...), condition=%wide.region_9.10_spmd.clone.clone, body=%wide.region_6.9_spmd.clone.clone.sunk | while | flops 1313740800 | bytes 13274933 | solution.py:82
  244.6 16.7 %dynamic_update_slice.83 = f32[2,256,12,64]{1,0,3,2:T(2,128)} dynamic-update-slice(f32[2,256,12,64]{1,0,3,2:T(2,128)} %get-tuple-element.1165, f32[1,256,12,64]{1,0,3,2:T(1,128)S(1)} %copy.307, s32[]{:T(128)S(6)} %copy.342, s32[]{:T(128)} %constant.147.clone.1..sunk, s32[]{:T(128)} %constant.147.clone.1..sunk, s32[]{:T(128)} %constant.147.clone.1..sunk) | dynamic-update-slice | bytes 1572868 | tf_op jit(solution)/shard_map/jvp()/while/body/jit(dynamic_update_index_in_dim)/dynamic_update_slice | solution.py:82
  274.1 16.7 %dynamic_update_slice.83 = f32[2,256,12,64]{1,0,3,2:T(2,128)} dynamic-update-slice(f32[2,256,12,64]{1,0,3,2:T(2,128)} %get-tuple-element.1165, f32[1,256,12,64]{1,0,3,2:T(1,128)S(1)} %copy.307, s32[]{:T(128)S(6)} %copy.342, s32[]{:T(128)} %constant.147.clone.1..sunk, s32[]{:T(128)} %constant.147.clone.1..sunk, s32[]{:T(128)} %constant.147.clone.1..sunk) | dynamic-update-slice | bytes 1572868 | tf_op jit(solution)/shard_map/jvp()/while/body/jit(dynamic_update_index_in_dim)/dynamic_update_slice | solution.py:82
  340.1 183.3 %while.66 = (s32[]{:T(128)}, f32[12,64,128]{2,1,0:T(8,128)}, f32[2,256,12,64]{1,0,3,2:T(2,128)}, f32[2,256,128]{2,1,0:T(8,128)}, f32[2,256,128]{2,1,0:T(8,128)},...) while((s32[]{:T(128)}, f32[12,64,128]{2,1,0:T(8,128)}, ...), condition=%wide.region_27.28_spmd.clone, body=%wide.region_15.27_spmd.clone.sunk | while | flops 3038771200 | bytes 46435668 | solution.py:82
  414.5 16.7 %dynamic_update_slice.88 = f32[2,256,12,64]{1,0,3,2:T(2,128)} dynamic-update-slice(f32[2,256,12,64]{1,0,3,2:T(2,128)} %get-tuple-element.1208, f32[1,256,12,64]{1,0,3,2:T(1,128)S(1)} %copy.320, s32[]{:T(128)S(6)} %sub.303, s32[]{:T(128)} %constant.147.clone.1..sunk.1, s32[]{:T(128)} %constant.147.clone.1..sunk.1, s32[]{:T(128)} %constant.147.clone.1..sunk.1) | dynamic-update-slice | bytes 1572868 | tf_op jit(solution)/shard_map/transpose(jvp())/while/body/jit(dynamic_update_index_in_dim)/dynamic_update_slice | solution.py:82
  506.6 16.7 %dynamic_update_slice.88 = f32[2,256,12,64]{1,0,3,2:T(2,128)} dynamic-update-slice(f32[2,256,12,64]{1,0,3,2:T(2,128)} %get-tuple-element.1208, f32[1,256,12,64]{1,0,3,2:T(1,128)S(1)} %copy.320, s32[]{:T(128)S(6)} %sub.303, s32[]{:T(128)} %constant.147.clone.1..sunk.1, s32[]{:T(128)} %constant.147.clone.1..sunk.1, s32[]{:T(128)} %constant.147.clone.1..sunk.1) | dynamic-update-slice | bytes 1572868 | tf_op jit(solution)/shard_map/transpose(jvp())/while/body/jit(dynamic_update_index_in_dim)/dynamic_update_slice | solution.py:82
  523.5 210.7 %while.64 = (s32[]{:T(128)}, f32[12,64,128]{2,1,0:T(8,128)S(1)}, f32[12]{0:T(128)}, f32[12,64,128]{2,1,0:T(8,128)}, s32[]{:T(128)}) while((s32[]{:T(128)}, f32[12,64,128]{2,1,0:T(8,128)S(1)}, f32[12]{0:T(128)}, f32[12,64,128]{2,1,0:T(8,128)}, s32[]{:T(128)}) %tuple.214), condition=%wide.region_29.30_spmd, body=%wide.region_28.29_spmd.sunk | while | flops 196610 | bytes 2752661 | solution.py:197
  526.7 10.2 collective-permute-done.1
  540.0 10.2 collective-permute-done.1
  553.3 10.2 collective-permute-done.1
  566.6 10.2 collective-permute-done.1
  580.0 9.7 collective-permute-done.1
  592.8 11.7 %collective-permute-done.1 = f32[12,64,128]{2,1,0:T(8,128)S(1)} collective-permute-done((f32[12,64,128]{2,1,0:T(8,128)}, f32[12,64,128]{2,1,0:T(8,128)S(1)}, u32[]{:S(2)}, u32[]{:S(2)}) %collective-permute-start.1) | collective-permute-done | bytes 393248 | tf_op jit(solution)/shard_map/while/body/eval_jaxpr/ppermute | solution.py:18
  607.7 17.1 %collective-permute-done.1 = f32[12,64,128]{2,1,0:T(8,128)S(1)} collective-permute-done((f32[12,64,128]{2,1,0:T(8,128)}, f32[12,64,128]{2,1,0:T(8,128)S(1)}, u32[]{:S(2)}, u32[]{:S(2)}) %collective-permute-start.1) | collective-permute-done | bytes 393248 | tf_op jit(solution)/shard_map/while/body/eval_jaxpr/ppermute | solution.py:18
  627.9 15.4 %collective-permute-done.1 = f32[12,64,128]{2,1,0:T(8,128)S(1)} collective-permute-done((f32[12,64,128]{2,1,0:T(8,128)}, f32[12,64,128]{2,1,0:T(8,128)S(1)}, u32[]{:S(2)}, u32[]{:S(2)}) %collective-permute-start.1) | collective-permute-done | bytes 393248 | tf_op jit(solution)/shard_map/while/body/eval_jaxpr/ppermute | solution.py:18
  646.5 12.6 %collective-permute-done.1 = f32[12,64,128]{2,1,0:T(8,128)S(1)} collective-permute-done((f32[12,64,128]{2,1,0:T(8,128)}, f32[12,64,128]{2,1,0:T(8,128)S(1)}, u32[]{:S(2)}, u32[]{:S(2)}) %collective-permute-start.1) | collective-permute-done | bytes 393248 | tf_op jit(solution)/shard_map/while/body/eval_jaxpr/ppermute | solution.py:18
  662.2 10.2 collective-permute-done.1
  675.6 9.5 collective-permute-done.1
  711.9 9.5 collective-permute-done.1
  724.6 9.5 collective-permute-done.1
  779.6 44.2 %all-reduce.17.cloned.1.call-done = f32[512,256]{1,0:T(8,128)} async-done(((f32[512,256]{1,0:T(8,128)}), f32[512,256]{1,0:T(8,128)}) %all-reduce.17.cloned.1.call-update) | async-done | bytes 524304 | tf_op jit(solution)/shard_map/psum | solution.py:210
  869.4 38.2 %reduce-scatter.5.cloned.1.call-done = f32[512,384]{1,0:T(8,128)} async-done(((f32[512,1536]{1,0:T(8,128)}), f32[512,384]{1,0:T(8,128)}) %reduce-scatter.5.cloned.1.call-update) | async-done | bytes 786448 | tf_op jit(solution)/shard_map/reduce_scatter | solution.py:240
  909.3 131.2 %all-reduce.12 = (f32[384]{0:T(512)}, f32[4,768]{1,0:T(4,128)}, f32[4,256]{1,0:T(4,128)}, f32[768]{0:T(1024)}, f32[256]{0:T(256)}, /*index=5*/f32[12]{0:T(128)}, f32[12]{0:T(128)}, f32[12]{0:T(128)}, f32[768]{0:T(1024)}) all-reduce(f32[384]{0:T(512)S(1)} %get-tuple-element.729, ...), channel_id=1, replica_groups=mesh['dp'=2,'seq'=16,'head'=4] {'dp','seq'}, use_global_device_ids=true, to_apply=%region_39.40 | all-reduce | flops 6308 | bytes 50464 | tf_op jit(solution)/shard_map/psum | solution.py:249
  (670 shorter events, 630.9 us)
Async XLA Ops:
  7.2 816.6 %all-reduce.17.cloned.1.call-start = ((), (), s32[]{:S(2)}) async-start(), calls=%async_computation.3 | async-start | bytes 1048576 | tf_op jit(solution)/shard_map/psum | solution.py:210
  14.2 12.3 %collective-permute-start.2 = (f32[3,1024]{1,0:T(4,128)}, f32[3,1024]{1,0:T(4,128)S(1)}, u32[]{:S(2)}, u32[]{:S(2)}) collective-permute-start(f32[3,1024]{1,0:T(4,128)} %pad_maximum_fusion.3), channel_id=1, source_target_pairs={{0,4},{4,8},{8,12},{12,16},{16,20},{20,24},{24,28},{28,32},{32,36}... | collective-permute-start | bytes 36872 | tf_op jit(solution)/shard_map/ppermute | solution.py:18
  40.2 11.3 %collective-permute-start = (f32[12,64,128]{2,1,0:T(8,128)}, f32[12,64,128]{2,1,0:T(8,128)S(1)}, u32[]{:S(2)}, u32[]{:S(2)}) collective-permute-start(f32[12,64,128]{2,1,0:T(8,128)} %multiply_add_fusion.10), channel_id=1, source_target_pairs={{0,4},{4,8},{8,12},{12,16},{16,20},{20,24},{24,28},{28,32},{32,36}... | collective-permute-start | bytes 1179656 | tf_op jit(solution)/shard_map/while/body/eval_jaxpr/ppermute | solution.py:18
  105.2 11.1 %collective-permute-start = (f32[12,64,128]{2,1,0:T(8,128)}, f32[12,64,128]{2,1,0:T(8,128)S(1)}, u32[]{:S(2)}, u32[]{:S(2)}) collective-permute-start(f32[12,64,128]{2,1,0:T(8,128)} %multiply_add_fusion.10), channel_id=1, source_target_pairs={{0,4},{4,8},{8,12},{12,16},{16,20},{20,24},{24,28},{28,32},{32,36}... | collective-permute-start | bytes 1179656 | tf_op jit(solution)/shard_map/while/body/eval_jaxpr/ppermute | solution.py:18
  128.8 11.3 %collective-permute-start = (f32[12,64,128]{2,1,0:T(8,128)}, f32[12,64,128]{2,1,0:T(8,128)S(1)}, u32[]{:S(2)}, u32[]{:S(2)}) collective-permute-start(f32[12,64,128]{2,1,0:T(8,128)} %multiply_add_fusion.10), channel_id=1, source_target_pairs={{0,4},{4,8},{8,12},{12,16},{16,20},{20,24},{24,28},{28,32},{32,36}... | collective-permute-start | bytes 1179656 | tf_op jit(solution)/shard_map/while/body/eval_jaxpr/ppermute | solution.py:18
  141.0 12.7 %collective-permute-start = (f32[12,64,128]{2,1,0:T(8,128)}, f32[12,64,128]{2,1,0:T(8,128)S(1)}, u32[]{:S(2)}, u32[]{:S(2)}) collective-permute-start(f32[12,64,128]{2,1,0:T(8,128)} %multiply_add_fusion.10), channel_id=1, source_target_pairs={{0,4},{4,8},{8,12},{12,16},{16,20},{20,24},{24,28},{28,32},{32,36}... | collective-permute-start | bytes 1179656 | tf_op jit(solution)/shard_map/while/body/eval_jaxpr/ppermute | solution.py:18
  154.5 14.0 %collective-permute-start = (f32[12,64,128]{2,1,0:T(8,128)}, f32[12,64,128]{2,1,0:T(8,128)S(1)}, u32[]{:S(2)}, u32[]{:S(2)}) collective-permute-start(f32[12,64,128]{2,1,0:T(8,128)} %multiply_add_fusion.10), channel_id=1, source_target_pairs={{0,4},{4,8},{8,12},{12,16},{16,20},{20,24},{24,28},{28,32},{32,36}... | collective-permute-start | bytes 1179656 | tf_op jit(solution)/shard_map/while/body/eval_jaxpr/ppermute | solution.py:18
  169.3 15.4 %collective-permute-start = (f32[12,64,128]{2,1,0:T(8,128)}, f32[12,64,128]{2,1,0:T(8,128)S(1)}, u32[]{:S(2)}, u32[]{:S(2)}) collective-permute-start(f32[12,64,128]{2,1,0:T(8,128)} %multiply_add_fusion.10), channel_id=1, source_target_pairs={{0,4},{4,8},{8,12},{12,16},{16,20},{20,24},{24,28},{28,32},{32,36}... | collective-permute-start | bytes 1179656 | tf_op jit(solution)/shard_map/while/body/eval_jaxpr/ppermute | solution.py:18
  185.5 15.4 %collective-permute-start = (f32[12,64,128]{2,1,0:T(8,128)}, f32[12,64,128]{2,1,0:T(8,128)S(1)}, u32[]{:S(2)}, u32[]{:S(2)}) collective-permute-start(f32[12,64,128]{2,1,0:T(8,128)} %multiply_add_fusion.10), channel_id=1, source_target_pairs={{0,4},{4,8},{8,12},{12,16},{16,20},{20,24},{24,28},{28,32},{32,36}... | collective-permute-start | bytes 1179656 | tf_op jit(solution)/shard_map/while/body/eval_jaxpr/ppermute | solution.py:18
  201.8 13.2 %collective-permute-start = (f32[12,64,128]{2,1,0:T(8,128)}, f32[12,64,128]{2,1,0:T(8,128)S(1)}, u32[]{:S(2)}, u32[]{:S(2)}) collective-permute-start(f32[12,64,128]{2,1,0:T(8,128)} %multiply_add_fusion.10), channel_id=1, source_target_pairs={{0,4},{4,8},{8,12},{12,16},{16,20},{20,24},{24,28},{28,32},{32,36}... | collective-permute-start | bytes 1179656 | tf_op jit(solution)/shard_map/while/body/eval_jaxpr/ppermute | solution.py:18
  215.8 11.3 %collective-permute-start = (f32[12,64,128]{2,1,0:T(8,128)}, f32[12,64,128]{2,1,0:T(8,128)S(1)}, u32[]{:S(2)}, u32[]{:S(2)}) collective-permute-start(f32[12,64,128]{2,1,0:T(8,128)} %multiply_add_fusion.10), channel_id=1, source_target_pairs={{0,4},{4,8},{8,12},{12,16},{16,20},{20,24},{24,28},{28,32},{32,36}... | collective-permute-start | bytes 1179656 | tf_op jit(solution)/shard_map/while/body/eval_jaxpr/ppermute | solution.py:18
  525.4 11.5 %collective-permute-start.1 = (f32[12,64,128]{2,1,0:T(8,128)}, f32[12,64,128]{2,1,0:T(8,128)S(1)}, u32[]{:S(2)}, u32[]{:S(2)}) collective-permute-start(f32[12,64,128]{2,1,0:T(8,128)} %multiply_add_fusion.11), channel_id=1, source_target_pairs={{4,0},{8,4},{12,8},{16,12},{20,16},{24,20},{28,24},{32,28},{36,32}... | collective-permute-start | bytes 1179656 | tf_op jit(solution)/shard_map/while/body/eval_jaxpr/ppermute | solution.py:18
  538.7 11.5 %collective-permute-start.1 = (f32[12,64,128]{2,1,0:T(8,128)}, f32[12,64,128]{2,1,0:T(8,128)S(1)}, u32[]{:S(2)}, u32[]{:S(2)}) collective-permute-start(f32[12,64,128]{2,1,0:T(8,128)} %multiply_add_fusion.11), channel_id=1, source_target_pairs={{4,0},{8,4},{12,8},{16,12},{20,16},{24,20},{28,24},{32,28},{36,32}... | collective-permute-start | bytes 1179656 | tf_op jit(solution)/shard_map/while/body/eval_jaxpr/ppermute | solution.py:18
  552.0 11.5 %collective-permute-start.1 = (f32[12,64,128]{2,1,0:T(8,128)}, f32[12,64,128]{2,1,0:T(8,128)S(1)}, u32[]{:S(2)}, u32[]{:S(2)}) collective-permute-start(f32[12,64,128]{2,1,0:T(8,128)} %multiply_add_fusion.11), channel_id=1, source_target_pairs={{4,0},{8,4},{12,8},{16,12},{20,16},{24,20},{28,24},{32,28},{36,32}... | collective-permute-start | bytes 1179656 | tf_op jit(solution)/shard_map/while/body/eval_jaxpr/ppermute | solution.py:18
  565.4 11.5 %collective-permute-start.1 = (f32[12,64,128]{2,1,0:T(8,128)}, f32[12,64,128]{2,1,0:T(8,128)S(1)}, u32[]{:S(2)}, u32[]{:S(2)}) collective-permute-start(f32[12,64,128]{2,1,0:T(8,128)} %multiply_add_fusion.11), channel_id=1, source_target_pairs={{4,0},{8,4},{12,8},{16,12},{20,16},{24,20},{28,24},{32,28},{36,32}... | collective-permute-start | bytes 1179656 | tf_op jit(solution)/shard_map/while/body/eval_jaxpr/ppermute | solution.py:18
  578.7 11.0 %collective-permute-start.1 = (f32[12,64,128]{2,1,0:T(8,128)}, f32[12,64,128]{2,1,0:T(8,128)S(1)}, u32[]{:S(2)}, u32[]{:S(2)}) collective-permute-start(f32[12,64,128]{2,1,0:T(8,128)} %multiply_add_fusion.11), channel_id=1, source_target_pairs={{4,0},{8,4},{12,8},{16,12},{20,16},{24,20},{28,24},{32,28},{36,32}... | collective-permute-start | bytes 1179656 | tf_op jit(solution)/shard_map/while/body/eval_jaxpr/ppermute | solution.py:18
  591.5 13.0 %collective-permute-start.1 = (f32[12,64,128]{2,1,0:T(8,128)}, f32[12,64,128]{2,1,0:T(8,128)S(1)}, u32[]{:S(2)}, u32[]{:S(2)}) collective-permute-start(f32[12,64,128]{2,1,0:T(8,128)} %multiply_add_fusion.11), channel_id=1, source_target_pairs={{4,0},{8,4},{12,8},{16,12},{20,16},{24,20},{28,24},{32,28},{36,32}... | collective-permute-start | bytes 1179656 | tf_op jit(solution)/shard_map/while/body/eval_jaxpr/ppermute | solution.py:18
  606.4 18.4 %collective-permute-start.1 = (f32[12,64,128]{2,1,0:T(8,128)}, f32[12,64,128]{2,1,0:T(8,128)S(1)}, u32[]{:S(2)}, u32[]{:S(2)}) collective-permute-start(f32[12,64,128]{2,1,0:T(8,128)} %multiply_add_fusion.11), channel_id=1, source_target_pairs={{4,0},{8,4},{12,8},{16,12},{20,16},{24,20},{28,24},{32,28},{36,32}... | collective-permute-start | bytes 1179656 | tf_op jit(solution)/shard_map/while/body/eval_jaxpr/ppermute | solution.py:18
  626.7 16.7 %collective-permute-start.1 = (f32[12,64,128]{2,1,0:T(8,128)}, f32[12,64,128]{2,1,0:T(8,128)S(1)}, u32[]{:S(2)}, u32[]{:S(2)}) collective-permute-start(f32[12,64,128]{2,1,0:T(8,128)} %multiply_add_fusion.11), channel_id=1, source_target_pairs={{4,0},{8,4},{12,8},{16,12},{20,16},{24,20},{28,24},{32,28},{36,32}... | collective-permute-start | bytes 1179656 | tf_op jit(solution)/shard_map/while/body/eval_jaxpr/ppermute | solution.py:18
  645.2 13.9 %collective-permute-start.1 = (f32[12,64,128]{2,1,0:T(8,128)}, f32[12,64,128]{2,1,0:T(8,128)S(1)}, u32[]{:S(2)}, u32[]{:S(2)}) collective-permute-start(f32[12,64,128]{2,1,0:T(8,128)} %multiply_add_fusion.11), channel_id=1, source_target_pairs={{4,0},{8,4},{12,8},{16,12},{20,16},{24,20},{28,24},{32,28},{36,32}... | collective-permute-start | bytes 1179656 | tf_op jit(solution)/shard_map/while/body/eval_jaxpr/ppermute | solution.py:18
  660.9 11.5 %collective-permute-start.1 = (f32[12,64,128]{2,1,0:T(8,128)}, f32[12,64,128]{2,1,0:T(8,128)S(1)}, u32[]{:S(2)}, u32[]{:S(2)}) collective-permute-start(f32[12,64,128]{2,1,0:T(8,128)} %multiply_add_fusion.11), channel_id=1, source_target_pairs={{4,0},{8,4},{12,8},{16,12},{20,16},{24,20},{28,24},{32,28},{36,32}... | collective-permute-start | bytes 1179656 | tf_op jit(solution)/shard_map/while/body/eval_jaxpr/ppermute | solution.py:18
  738.7 128.5 %reduce-scatter.3.cloned.1.call-start = ((), (), s32[]{:S(2)}) async-start(), calls=%async_computation.2 | async-start | bytes 3932160 | tf_op jit(solution)/shard_map/reduce_scatter | solution.py:178
  743.9 163.7 %reduce-scatter.5.cloned.1.call-start = ((), (), s32[]{:S(2)}) async-start(), calls=%async_computation.4 | async-start | bytes 3932160 | tf_op jit(solution)/shard_map/reduce_scatter | solution.py:240
  836.2 219.6 %all-reduce.19.cloned.1.call-start = ((), (), s32[]{:S(2)}) async-start(), calls=%async_computation.5 | async-start | bytes 29294592 | tf_op jit(solution)/shard_map/psum | solution.py:249
  (166 other events, 1819.0 us)
Sparse Core Ops, SparseCore 0:
  738.8 84.9 all-reduce.16
  826.2 40.9 reduce-scatter.2
  869.6 37.9 reduce-scatter.4
  912.7 142.9 all-reduce.18
where the time goes:
time: 1090 us; the launch traced here: 1070 us
  waiting for transfers between devices  356 us (33%)
  local copies, waits for them, and re-layouts  190 us (17%)
  blocking collectives  153 us (14%)
  other arithmetic  128 us (12%)
  matrix products  126 us (12%)
  starting transfers between devices  105 us (10%)
  between operations  15.3 us (1%)
    ppermute x32, waiting for transfers between devices, from_behind(): return lax.ppermute(shard, axis, pairs)  261 us
    psum x1, blocking collectives, per_device(): lax.psum((grad_norm_gain, grad_w_z, grad_w_x, grad_w_bc, grad_w_dt, grad_...  131 us
    ppermute x32, starting transfers between devices, from_behind(): return lax.ppermute(shard, axis, pairs)  105 us
    dynamic_update_slice x12, local copies, waits for them, and re-layouts, ssd_outputs(): lax.scan(jax.checkpoint(block_step), start_state, (split_rows(values), sp...  72.9 us
    psum x1, waiting for transfers between devices, per_device(): lax.psum(jnp.concatenate([grad_keys, grad_reads], axis=1), 'head')  44.2 us
    reduce_scatter x1, waiting for transfers between devices, per_device(): lax.psum_scatter(grad_normed, 'head', scatter_dimension=1, tiled=True)  38.2 us
    dot_general x6, matrix products, block_step(): within = jnp.einsum('hts,shp->thp', mixing, values, precision=highest)  32.6 us
    add x15, other arithmetic, backward_turn(): decay_here[:, None, None] * received + own_back  27.8 us
  transfers between devices with their start and end apart: 36, of which 35 were waited for; matrix products, arithmetic and copies ran while one was open for 8% of the time, Pallas kernels for 0%

commit v1 on v0

v1 whole, which is shorter than its diff:
```python
import functools

import jax
import jax.numpy as jnp
from jax import lax
from jax.experimental import pallas as pl
from jax.experimental.pallas import tpu as pltpu
from jax.sharding import PartitionSpec as P

HEADDIM = 64
STATE = 128
CHUNK = 128
LANES = 128
EDGE = 8

epsilon = 1e-05
f32 = jnp.float32
bf16 = jnp.bfloat16


def low(value):
    return value.astype(bf16)


def dot(left, right):
    return jnp.dot(left, right, preferred_element_type=f32)


def dot_nt(left, right):
    return lax.dot_general(left, right, (((1,), (1,)), ((), ())), preferred_element_type=f32)


def dot_tn(left, right):
    return lax.dot_general(left, right, (((0,), (0,)), ((), ())), preferred_element_type=f32)


def parts_of(value, count):
    terms = []
    for _ in range(count):
        term = value.astype(bf16)
        terms.append(term)
        value = value - term.astype(f32)
    return terms


def head_map(width):
    head = lax.broadcasted_iota(jnp.int32, (LANES, width), 0)
    column = lax.broadcasted_iota(jnp.int32, (LANES, width), 1)
    return (lax.shift_right_logical(column, 6) == head).astype(f32).astype(bf16)


def spread(per_head, heads):
    high, rest = parts_of(per_head, 2)
    return dot(high, heads) + dot(rest, heads)


def per_head_sum(channels, heads):
    high, rest = parts_of(channels, 2)
    return dot_nt(high, heads) + dot_nt(rest, heads)


def running(mask, value):
    terms = parts_of(value, 3)
    return dot(mask, terms[0]) + dot(mask, terms[1]) + dot(mask, terms[2])


def as_row(vector):
    return vector[...].reshape(1, vector.shape[0])


def row_col():
    row = lax.broadcasted_iota(jnp.int32, (CHUNK, CHUNK), 0)
    column = lax.broadcasted_iota(jnp.int32, (CHUNK, CHUNK), 1)
    return row, column


def as_mask(where):
    return where.astype(f32).astype(bf16)


def sigmoid(value):
    return 1.0 / (1.0 + jnp.exp(-value))


def silu(value):
    return value * sigmoid(value)


def silu_slope(value):
    sigma = sigmoid(value)
    return sigma * (1.0 + value * (1.0 - sigma))


def softplus(value):
    return jnp.maximum(value, 0.0) + jnp.log1p(jnp.exp(-jnp.abs(value)))


def column_sum(value):
    return jnp.sum(value, axis=0, keepdims=True)


def row_sum(value):
    return jnp.sum(value, axis=1, keepdims=True)


def exp_below(where, value):
    return jnp.exp(jnp.where(where, value, -1e30))


def project_kernel(hid, gain, wx, wbc, wdt, normed, normed32, inx, inbc, sraw, edge):
    rows = hid[...].astype(f32)
    scale = lax.rsqrt(jnp.mean(rows * rows, axis=1, keepdims=True) + epsilon)
    value = low(rows * scale * as_row(gain))
    normed[...] = value
    normed32[...] = value.astype(f32)
    width = inx.shape[1]
    inx[...] = dot(value, wx[...])
    inbc[...] = dot(value, wbc[...])
    edge[:, :width] = inx[CHUNK - EDGE :, :]
    edge[:, width:] = inbc[CHUNK - EDGE :, :]
    sraw[...] = jnp.zeros(sraw.shape, f32)
    sraw[:, : wdt.shape[0]] = dot_nt(value, wdt[...])


def conv_rows(ext, taps, bias):
    total = as_row(bias) + taps[0:1, :] * ext[pl.ds(EDGE - 3, CHUNK), :]
    for k in range(1, 4):
        total = total + taps[k : k + 1, :] * ext[pl.ds(EDGE - 3 + k, CHUNK), :]
    return total


def front_kernel(
    edge, inx, inbc, sraw, cx, cbc, bx, bbc, small,
    prex, prebc, step_out, cumc_out, cumd_out, starts, payload,
    extx, extbc, state, base,
):
    i = pl.program_id(0)
    width = inx.shape[1]

    @pl.when(i == 0)
    def _():
        extx[0:EDGE, :] = edge[:, :width]
        extbc[0:EDGE, :] = edge[:, width:]
        state[...] = jnp.zeros(state.shape, f32)
        base[...] = jnp.zeros(base.shape, f32)

    @pl.when(i > 0)
    def _():
        extx[0:EDGE, :] = extx[CHUNK : CHUNK + EDGE, :]
        extbc[0:EDGE, :] = extbc[CHUNK : CHUNK + EDGE, :]

    extx[EDGE:, :] = inx[...]
    extbc[EDGE:, :] = inbc[...]
    pre_x = conv_rows(extx, cx, bx)
    pre_bc = conv_rows(extbc, cbc, bbc)
    prex[...] = pre_x
    prebc[...] = pre_bc
    values = low(silu(pre_x)).astype(f32)
    keys_t = jnp.transpose(low(silu(pre_bc[:, :STATE])).astype(f32))
    step = softplus(sraw[...] + small[0:1, :])
    decay = -jnp.exp(small[1:2, :]) * step
    row, column = row_col()
    cumc = running(as_mask(row >= column), decay)
    last = cumc[CHUNK - 1 : CHUNK, :]
    step_out[...] = step
    cumc_out[...] = cumc
    cumd_out[...] = cumc + base[0:1, :]
    starts[0] = state[...]
    heads = head_map(width)
    weights = spread(jnp.exp(last - cumc) * step, heads)
    keep = spread(jnp.exp(jnp.broadcast_to(last, (EDGE, LANES))), heads)[0:1, :]
    state[...] = keep * state[...] + dot(low(keys_t), low(values * weights))
    base[...] = base[...] + last

    @pl.when(i == pl.num_programs(0) - 1)
    def _():
        payload[:, :width] = state[...]
        payload[:, width:] = jnp.broadcast_to(base[0:1, :], (STATE, LANES))


def scan_kernel(parts, ranges, received, incoming, decays):
    width = incoming.shape[1]
    decays[...] = spread(jnp.exp(received[:, width:]), head_map(width))
    carry = jnp.zeros((parts, width), f32)
    for i in range(ranges):
        here = slice(i * parts, (i + 1) * parts)
        incoming[here, :] = carry
        carry = decays[here, :] * carry + received[here, :width]


def scan_back_kernel(parts, ranges, received, decays, incoming):
    carry = jnp.zeros((parts, incoming.shape[1]), f32)
    for i in reversed(range(ranges)):
        here = slice(i * parts, (i + 1) * parts)
        incoming[here, :] = carry
        carry = decays[here, :] * carry + received[here, :]


def within_kernel(prex, prebc, step_in, cumc_in, starts, out):
    width = prex.shape[1]
    heads = head_map(width)
    values = low(silu(prex[...])).astype(f32)
    act_bc = low(silu(prebc[...]))
    keys, reads = act_bc[:, :STATE], act_bc[:, STATE:]
    step, cumc = step_in[...], cumc_in[...]
    cum_t = jnp.transpose(cumc)
    scaled = values * spread(step, heads)
    carried = spread(jnp.exp(cumc), heads) * dot(reads, low(starts[0]))
    scores = dot_nt(reads, keys)
    row, column = row_col()
    causal = row >= column
    first = lax.broadcasted_iota(jnp.int32, (CHUNK, LANES), 1) < HEADDIM
    for pair in range(width // LANES):
        lanes = slice(pair * LANES, (pair + 1) * LANES)
        pieces = []
        for h in (2 * pair, 2 * pair + 1):
            decayed = exp_below(causal, cumc[:, h : h + 1] - cum_t[h : h + 1, :])
            pieces.append(low(decayed * scores))
        here = scaled[:, lanes]
        stacked = jnp.concatenate(
            [low(jnp.where(first, here, 0.0)), low(jnp.where(first, 0.0, here))], axis=0
        )
        out[:, lanes] = carried[:, lanes] + dot(jnp.concatenate(pieces, axis=1), stacked)


def mix_kernel(incoming, prex, prebc, cumd, within, gate_z, d_out, small, gain, mixed_out, sums):
    width = prex.shape[1]
    heads = head_map(width)
    reads = low(silu(prebc[:, STATE:]))
    ssd = within[...] + spread(jnp.exp(cumd[...]), heads) * dot(reads, low(incoming[...]))
    skip = spread(small[...], heads)[2:3, :]
    mixed = ssd + skip * silu(prex[...])
    mixed_out[...] = mixed
    gated = mixed * silu(gate_z[...])
    squares = row_sum(gated * gated)
    products = row_sum(d_out[...] * as_row(gain) * gated)
    column = lax.broadcasted_iota(jnp.int32, (CHUNK, LANES), 1)
    both = jnp.where(column == 0, squares, jnp.where(column == 1, products, 0.0))
    sums[...] = jnp.broadcast_to(jnp.transpose(both)[0:2, :][None], sums.shape)


def gate_kernel(
    inner_all, totals, mixed_in, gate_z, d_out, prex, prebc, cumd, small, gain,
    normed_out, gate_low, d_mixed, col_out, payload,
):
    i = pl.program_id(0)
    width = prex.shape[1]
    heads = head_map(width)

    @pl.when(i == 0)
    def _():
        col_out[...] = jnp.zeros(col_out.shape, f32)
        payload[...] = jnp.zeros(payload.shape, f32)

    all_sums = totals[0]
    for k in range(1, totals.shape[0]):
        all_sums = all_sums + totals[k]
    squares, products = (
        jnp.transpose(jnp.broadcast_to(all_sums[r : r + 1, :], (CHUNK, CHUNK)))[:, 0:1]
        for r in range(2)
    )
    scale = lax.rsqrt(squares / inner_all + epsilon)
    mean_dot = scale * products / inner_all
    gate = gate_z[...]
    sigma = sigmoid(gate)
    silu_z = gate * sigma
    mixed = mixed_in[...]
    unit = mixed * silu_z * scale
    d_normed = d_out[...]
    gain_row = as_row(gain)
    out_low = low(unit * gain_row)
    normed_out[...] = out_low
    d_gated = scale * (d_normed * gain_row - unit * mean_dot)
    g_low = low(d_gated * silu_z)
    d_mixed[...] = g_low
    slope = sigma * (1.0 + gate * (1.0 - sigma))
    gate_grad = low(d_gated * mixed * slope)
    gate_low[...] = gate_grad
    g = g_low.astype(f32)
    col_out[0:1, :] += column_sum(d_normed * unit)
    col_out[1:2, :] += column_sum(g * silu(prex[...]))
    reads_t = jnp.transpose(low(silu(prebc[:, STATE:])).astype(f32))
    payload[...] += dot(low(reads_t), low(g * spread(jnp.exp(cumd[...]), heads)))


def back_kernel(
    prex, prebc, step_in, cumc_in, cumd, starts, incoming, d_mixed,
    d_values, d_bc, d_step, d_log, full_starts,
    later, gy_t,
):
    i = pl.program_id(0)
    width = prex.shape[1]
    heads = head_map(width)

    @pl.when(i == 0)
    def _():
        later[...] = jnp.zeros(later.shape, f32)
        gy_t[...] = jnp.zeros(gy_t.shape, f32)

    values_low = low(silu(prex[...]))
    values = values_low.astype(f32)
    act_bc = low(silu(prebc[...]))
    keys, reads = act_bc[:, :STATE], act_bc[:, STATE:]
    step, cumc = step_in[...], cumc_in[...]
    cum_t = jnp.transpose(cumc)
    last = cumc[CHUNK - 1 : CHUNK, :]
    before = cumd[CHUNK - 1 : CHUNK, :] - last
    tops = jnp.concatenate(
        [jnp.broadcast_to(before, (EDGE, LANES)), jnp.broadcast_to(last, (EDGE, LANES))], axis=0
    )
    tops = spread(jnp.exp(tops), heads)
    start = starts[0] + tops[0:1, :] * incoming[...]
    full_starts[0] = start
    keep = tops[EDGE : EDGE + 1, :]
    start_low = low(start)
    step_wide = spread(step, heads)
    out_wide = spread(jnp.exp(last - cumc), heads)
    g_low = d_mixed[...]
    g = g_low.astype(f32)
    g_in = g * spread(jnp.exp(cumc), heads)
    g_in_low = low(g_in)

    row, column = row_col()
    causal = row <= column
    scores_t = dot_nt(keys, reads)
    first = lax.broadcasted_iota(jnp.int32, (CHUNK, LANES), 1) < HEADDIM
    d_scores_t = jnp.zeros((CHUNK, CHUNK), f32)
    step_within = jnp.zeros((CHUNK, LANES), f32)
    later_low = low(later[...])
    onward = out_wide * dot(keys, later_low)
    for pair in range(width // LANES):
        lanes = slice(pair * LANES, (pair + 1) * LANES)
        g_pair = g[:, lanes]
        halves = (low(jnp.where(first, g_pair, 0.0)), low(jnp.where(first, 0.0, g_pair)))
        pieces = []
        for h, g_half in zip((2 * pair, 2 * pair + 1), halves):
            decayed = exp_below(causal, cum_t[h : h + 1, :] - cumc[:, h : h + 1])
            d_mixing = dot_nt(values_low[:, lanes], g_half)
            weighted = decayed * d_mixing
            step_col = step[:, h : h + 1]
            d_scores_t = d_scores_t + weighted * step_col
            product = weighted * scores_t
            step_within = step_within + jnp.where(column == h, row_sum(product), 0.0)
            gy_t[h : h + 1, :] = column_sum(product * step_col)
            pieces.append(low(decayed * scores_t))
        d_pair = dot(jnp.concatenate(pieces, axis=1), jnp.concatenate(halves, axis=0))
        d_values[:, lanes] = step_wide[:, lanes] * (d_pair + onward[:, lanes])

    d_keys = dot(low(d_scores_t), reads) + dot_nt(low(values * step_wide * out_wide), later_low)
    d_reads = dot(low(jnp.transpose(d_scores_t)), keys) + dot_nt(g_in_low, start_low)
    d_bc[:, :STATE] = d_keys
    d_bc[:, STATE:] = d_reads
    from_start = per_head_sum(g_in * dot(reads, start_low), heads)
    step_onward = per_head_sum(values * onward, heads)
    d_step[...] = step_within + step_onward
    across = column_sum(start * later[...])
    across = per_head_sum(jnp.broadcast_to(across, (EDGE, width)), heads)[0:1, :] * jnp.exp(last)
    inside = jnp.transpose(gy_t[...]) - step * step_within + from_start
    d_log[...] = (
        running(as_mask(row <= column), inside)
        + running(as_mask(row > column), step * step_onward)
        + across
    )
    later[...] = keep * later[...] + dot(low(jnp.transpose(reads.astype(f32))), g_in_low)


def edge_kernel(incoming, prex, prebc, step_in, cumd, total, d_mixed, d_values, d_bc, small, out):
    width = prex.shape[1]
    heads = head_map(width)
    low_in = low(incoming[...])
    act_bc = low(silu(prebc[...]))
    step = step_in[...]
    weight = spread(step * jnp.exp(total[EDGE - 1 : EDGE, :] - cumd[...]), heads)
    skip = spread(small[...], heads)[2:3, :]
    values = low(silu(prex[...])).astype(f32)
    d_val = d_values[...] + weight * dot(act_bc[:, :STATE], low_in)
    d_keys = d_bc[:, :STATE] + dot_nt(low(values * weight), low_in)
    d_act = d_val + skip * d_mixed[...].astype(f32)[:EDGE]
    out[:, :width] = d_act * silu_slope(prex[...])
    out[:, width : width + STATE] = d_keys * silu_slope(prebc[:, :STATE])
    out[:, width + STATE :] = d_bc[:, STATE:] * silu_slope(prebc[:, STATE:])


def conv_back(chunk, ext, inner, before, edge, taps, d_pre, sums, columns):
    ext[0:CHUNK, :] = d_pre
    d_inner = taps[3:4, :] * d_pre
    for k in range(3):
        d_inner = d_inner + taps[k : k + 1, :] * ext[pl.ds(3 - k, CHUNK), :]
    ext[CHUNK:, :] = ext[0:EDGE, :]
    rows = jnp.where(chunk == 0, edge, before[...])
    inner[0:EDGE, :] = rows
    for k in range(4):
        sums[k : k + 1, columns] += column_sum(d_pre * inner[pl.ds(EDGE - 3 + k, CHUNK), :])
    sums[4:5, columns] += column_sum(d_pre)
    return d_inner


def finish_kernel(
    core, incoming, full_starts, prex, prebc, inx, inbc, before_x, before_bc, edge, edge_next,
    sraw, step_in, cumc_in, cumd_in, total, d_mixed, d_values, d_bc, d_step, d_log, cx, cbc, small,
    col_in,
    x_low, own, send, bc_low, bc_rows, step_out, sums,
    ext_x, ext_bc, inner_x, inner_bc,
):
    i = pl.program_id(0)
    chunk = pl.num_programs(0) - 1 - i
    width = prex.shape[1]
    half = width // 2
    heads = head_map(width)

    @pl.when(i == 0)
    def _():
        ext_x[CHUNK:, :] = edge_next[:, :width]
        ext_bc[CHUNK:, :] = edge_next[:, width:]
        sums[...] = jnp.zeros(sums.shape, f32)
        sums[5:7, :width] = col_in[0:2, :]

    late = incoming[...]
    late_low = low(late)
    act_bc = low(silu(prebc[...]))
    keys = act_bc[:, :STATE]
    pre_x = prex[...]
    sigma = sigmoid(pre_x)
    slope_x = sigma * (1.0 + pre_x * (1.0 - sigma))
    values = low(pre_x * sigma).astype(f32)
    step, cumd = step_in[...], cumd_in[...]
    end = total[EDGE - 1 : EDGE, :]
    step_wide = spread(step, heads)
    out_wide = spread(jnp.exp(end - cumd), heads)
    skip = spread(small[...], heads)[2:3, :]
    onward = out_wide * dot(keys, late_low)
    d_val = d_values[...] + step_wide * onward
    d_keys = d_bc[:, :STATE] + dot_nt(low(values * step_wide * out_wide), late_low)
    step_onward = per_head_sum(values * onward, heads)
    before = cumd[CHUNK - 1 : CHUNK, :] - cumc_in[CHUNK - 1 : CHUNK, :]
    across = column_sum(full_starts[0] * late)
    across = per_head_sum(jnp.broadcast_to(across, (EDGE, width)), heads)[0:1, :]
    row, column = row_col()
    log_grad = (
        d_log[...]
        + running(as_mask(row > column), step * step_onward)
        + across * jnp.exp(end - before)
    )
    rate = jnp.exp(small[1:2, :])
    step_grad = d_step[...] + step_onward - rate * log_grad
    raw = sraw[...] + small[0:1, :]
    step_pre = step_grad * sigmoid(raw)
    for_heads = slice(width + 2 * STATE, width + 2 * STATE + LANES)
    sums[0:1, for_heads] += column_sum(log_grad * (-rate * step))
    sums[1:2, for_heads] += column_sum(step_pre)
    step_out[...] = low(step_pre)

    d_pre_x = (d_val + skip * d_mixed[...].astype(f32)) * slope_x
    inner_x[EDGE:, :] = inx[...]
    of_x = slice(0, width)
    d_in = low(
        conv_back(chunk, ext_x, inner_x, before_x, edge[:, of_x], cx, d_pre_x, sums, of_x)
    )
    x_low[...] = d_in
    wide = d_in.astype(f32)
    is_first = core[0] == 0
    own[...] = low(jnp.where(is_first, wide[:, :half], wide[:, half:]))
    send[...] = jnp.where(is_first, wide[:, half:], wide[:, :half])

    d_act_bc = jnp.concatenate([d_keys, d_bc[:, STATE:]], axis=1)
    d_pre_bc = d_act_bc * silu_slope(prebc[...])
    inner_bc[EDGE:, :] = inbc[...]
    of_bc = slice(width, width + 2 * STATE)
    d_in = conv_back(
        chunk, ext_bc, inner_bc, before_bc, edge[:, of_bc], cbc, d_pre_bc, sums, of_bc
    )
    bc_low[...] = low(d_in)
    shares = jnp.transpose(d_in)
    share = bc_rows.shape[1]
    for k in range(bc_rows.shape[0]):
        bc_rows[k] = shares[k * share : (k + 1) * share, :]


def norm_back_kernel(
    dg, dx, dbc, dst, ahead, hid, hid_block, gain, wz, wx, wbc, wdt, wout, sums, bc_rows, out, parts, scale, along, gains
):
    i = pl.program_id(0)
    last = pl.num_programs(0) - 1
    _, count, width = out.shape

    @pl.when(i == 0)
    def _():
        rows = hid[...].astype(f32)
        mean = jnp.mean(rows * rows, axis=1, keepdims=True)
        scale[...] = jnp.broadcast_to(lax.rsqrt(mean + epsilon), scale.shape)
        along[...] = jnp.zeros(along.shape, f32)

    total = dot_nt(dg[...], wz[...]) + dot_nt(dx[...], wx[...])
    total = total + dot_nt(dbc[...], wbc[...])
    total = total + dot(dst[:, : wdt.shape[0]], wdt[...])
    out[0] = dot(ahead[...], wout[...])
    out[1] = total
    product = total * (hid_block[...].astype(f32) * scale[:, 0:1])
    here = pl.ds(pl.multiple_of(i * width, width), width)
    gains[0:1, here] = column_sum(product)
    weighted = product * as_row(gain)
    partial = weighted[:, :LANES]
    for k in range(1, width // LANES):
        partial = partial + weighted[:, k * LANES : (k + 1) * LANES]
    along[...] += partial

    @pl.when(i == last)
    def _():
        heads, share = bc_rows.shape[0], bc_rows.shape[1]
        first = dg.shape[1]
        own = gains.shape[1] // heads
        parts[...] = jnp.zeros(parts.shape, f32)
        for k in range(heads):
            parts[k, :share, :] = bc_rows[k]
            parts[k, share : share + 5, : 2 * STATE] = sums[0:5, first : first + 2 * STATE]
            parts[k, share + 5 : share + 6, :own] = gains[0:1, k * own : (k + 1) * own]
        for j in range(count // CHUNK):
            lanes = slice(j * CHUNK, (j + 1) * CHUNK)
            line = column_sum(jnp.transpose(along[lanes, :]))
            for k in range(heads):
                parts[k, share + 6 : share + 7, lanes] = line


def share_kernel(buffer, parts, step_low, normed, sums, out, dots):
    share = parts[0]
    for k in range(1, parts.shape[0]):
        share = share + parts[k]
    count = share.shape[0] - EDGE
    extra = share[count:, :]
    dots[...] = extra
    features = normed.shape[1]
    own = features // parts.shape[0]
    width = features // 2
    gains = jnp.concatenate([extra[5:6, :own], jnp.zeros((1, features - own), f32)], axis=1)
    lane = lax.broadcasted_iota(jnp.int32, (EDGE, features), 1)
    row = lax.broadcasted_iota(jnp.int32, (EDGE, features), 0)
    of_bc = (lane >= width) & (lane < width + 2 * STATE) & (row < 5)
    summed = jnp.concatenate(
        [
            jnp.zeros((EDGE, width), f32),
            extra[:, : 2 * STATE],
            jnp.zeros((EDGE, features - width - 2 * STATE), f32),
        ],
        axis=1,
    )
    tiny = jnp.where(row == 7, gains, jnp.where(of_bc, summed, sums[...]))
    steps = 2 * EDGE
    of_w = dot(low(share[:count, :]), normed[...])
    of_dt = dot_tn(step_low[...], normed[...])[:steps, :]
    ranges, rows, half = out.shape
    spare = jnp.zeros((rows * ranges * half // features - count - steps - EDGE, features), f32)
    stacked = jnp.concatenate([of_w, of_dt, tiny, spare], axis=0)
    blocks = features // half
    per = ranges // blocks
    for k in range(blocks):
        out[k * per : (k + 1) * per] = stacked[:, k * half : (k + 1) * half].reshape(per, rows, half)


def copy_kernel(source, out):
    out[...] = source[...]


def join_kernel(core, mine, theirs, out):
    half = mine.shape[2]
    per = mine.shape[0]
    count = out.shape[0] // per
    own = mine[:, :count, :].reshape(per * count, half)
    other = theirs[:, :count, :].reshape(per * count, half)
    out[:, :half] = jnp.where(core[0] == 0, own, other)
    out[:, half:] = jnp.where(core[0] == 0, other, own)


def deal_kernel(
    mine, theirs, bc, dt, conv_x, conv_bc, bias_x, bias_bc, gain, norm_gain, by_head, sums
):
    share, steps = bc.shape[0], dt.shape[0]
    taps, width = conv_x.shape
    bc_width = conv_bc.shape[1]
    total = mine[...] + theirs[...]
    ranges, count, half = total.shape
    blocks = bc.shape[1] // half
    per = ranges // blocks
    first = share + 2 * EDGE
    for k in range(blocks):
        lanes = slice(k * half, (k + 1) * half)
        block = total[k * per : (k + 1) * per].reshape(per * count, half)
        bc[:, lanes] = block[:share, :]
        dt[:, lanes] = block[share : share + steps, :]
        sums[:, lanes] = block[first : first + EDGE, :]
    conv_x[...] = sums[:taps, :width]
    bias_x[...] = sums[taps, :width]
    conv_bc[...] = sums[:taps, width : width + bc_width]
    bias_bc[...] = sums[taps, width : width + bc_width]
    gain[...] = sums[5, :width]
    norm_gain[...] = sums[7, : norm_gain.shape[0]]
    by_head[...] = sums[:, width + bc_width : width + bc_width + LANES]
    by_head[2:3, :] = per_head_sum(sums[:, :width], head_map(width))[6:7, :]


def product_kernel(left, right, out):
    out[...] = dot_tn(left[...], right[...])


def outer_kernel(left, right, left_peer, right_peer, out):
    product = dot_tn(left[...], right[...]) + dot_tn(low(left_peer[...]), low(right_peer[...]))
    per, _, half = out.shape
    count = product.shape[0] // per
    out[:, :count, :] = product.reshape(per, count, half)


def total_kernel(parts, out):
    total = parts[0]
    for k in range(1, parts.shape[0]):
        total = total + parts[k]
    out[...] = jnp.broadcast_to(total[None], out.shape)


def whole(shape):
    return pl.BlockSpec(shape, lambda i: (0,) * len(shape))


def call(kernel, grid, ins, outs, scratch=(), flops=0, moved=0, megabytes=58, aliases=None):
    return pl.pallas_call(
        kernel,
        grid=(grid,),
        in_specs=[spec for _, spec in ins],
        out_specs=[spec for _, _, spec in outs],
        out_shape=[jax.ShapeDtypeStruct(shape, kind) for shape, kind, _ in outs],
        scratch_shapes=list(scratch),
        input_output_aliases=aliases or {},
        compiler_params=pltpu.CompilerParams(
            dimension_semantics=("arbitrary",), vmem_limit_bytes=megabytes * 2**20
        ),
        cost_estimate=pl.CostEstimate(flops=flops, bytes_accessed=moved, transcendentals=0),
    )(*[array for array, _ in ins])


def from_behind(shard, axis, by):
    peers = lax.axis_size(axis)
    pairs = [(i, i + by) for i in range(peers) if 0 <= i + by < peers]
    return lax.ppermute(shard, axis, pairs)


def swap_cores(shard):
    return lax.ppermute(shard, "dp", [(0, 1), (1, 0)])


def per_device(
    hidden,
    cotangent,
    norm_gain,
    w_z,
    w_x,
    w_bc,
    w_dt,
    conv_x,
    conv_bc,
    bias_x,
    bias_bc,
    dt_bias,
    a_log,
    skip_d,
    gain_out,
    w_out,
):
    hid, cot = hidden[0], cotangent[0]
    tokens, model_width = hid.shape
    heads_here = w_dt.shape[1]
    width = w_z.shape[1]
    half = width // 2
    bc_width = w_bc.shape[1]
    parts_head = lax.axis_size("head")
    bc_share = bc_width // parts_head
    chunks = tokens // CHUNK
    ranges = lax.axis_size("seq")
    parts = STATE // ranges
    head_pos = lax.axis_index("head")
    core = lax.axis_index("dp").astype(jnp.int32)
    core_flag = core.reshape(1)
    flag_spec = pl.BlockSpec(memory_space=pltpu.SMEM)

    def rows_of(count, columns):
        return pl.BlockSpec((count, columns), lambda i: (i, 0))

    def rows(columns):
        return rows_of(CHUNK, columns)

    def rows_back(columns):
        return pl.BlockSpec((CHUNK, columns), lambda i: (chunks - 1 - i, 0))

    pair_line = pl.BlockSpec((parts_head, 2, CHUNK), lambda i: (0, 0, i))
    state_spec = pl.BlockSpec((1, STATE, width), lambda i: (i, 0, 0))
    state_back = pl.BlockSpec((1, STATE, width), lambda i: (chunks - 1 - i, 0, 0))
    dt_rows = w_dt.T
    small = jnp.pad(
        jnp.stack([dt_bias, a_log, skip_d]), ((0, EDGE - 3), (0, LANES - heads_here))
    )
    small_spec = whole((EDGE, LANES))

    normed, normed32, inner_x, inner_bc, step_raw, edge = call(
        project_kernel,
        chunks,
        [
            (hid, rows(model_width)),
            (norm_gain, whole((model_width,))),
            (w_x, whole(w_x.shape)),
            (w_bc, whole(w_bc.shape)),
            (dt_rows, whole(dt_rows.shape)),
        ],
        [
            ((tokens, model_width), bf16, rows(model_width)),
            ((tokens, model_width), f32, rows(model_width)),
            ((tokens, width), f32, rows(width)),
            ((tokens, bc_width), f32, rows(bc_width)),
            ((tokens, LANES), f32, rows(LANES)),
            ((EDGE, width + bc_width), f32, whole((EDGE, width + bc_width))),
        ],
        flops=2 * tokens * model_width * (width + bc_width),
        moved=18 << 20,
    )
    edge = from_behind(edge, "seq", 1)
    gate_z = jnp.dot(normed, w_z, preferred_element_type=f32)
    d_out = jnp.einsum("td,id->ti", cot, w_out, preferred_element_type=f32)
    normed_peer = swap_cores(normed32)

    pre_x, pre_bc, step, cumc, cumd, starts, payload = call(
        front_kernel,
        chunks,
        [
            (edge, whole((EDGE, width + bc_width))),
            (inner_x, rows(width)),
            (inner_bc, rows(bc_width)),
            (step_raw, rows(LANES)),
            (conv_x, whole(conv_x.shape)),
            (conv_bc, whole(conv_bc.shape)),
            (bias_x, whole((width,))),
            (bias_bc, whole((bc_width,))),
            (small, small_spec),
        ],
        [
            ((tokens, width), f32, rows(width)),
            ((tokens, bc_width), f32, rows(bc_width)),
            ((tokens, LANES), f32, rows(LANES)),
            ((tokens, LANES), f32, rows(LANES)),
            ((tokens, LANES), f32, rows(LANES)),
            ((chunks, STATE, width), f32, state_spec),
            ((STATE, width + LANES), f32, whole((STATE, width + LANES))),
        ],
        [
            pltpu.VMEM((CHUNK + EDGE, width), f32),
            pltpu.VMEM((CHUNK + EDGE, bc_width), f32),
            pltpu.VMEM((STATE, width), f32),
            pltpu.VMEM((EDGE, LANES), f32),
        ],
        flops=2 * tokens * STATE * width,
        moved=8 << 20,
    )

    def exchanged(array):
        blocks = array.reshape(ranges, parts, array.shape[1])
        return lax.all_to_all(blocks, "seq", 0, 0).reshape(array.shape)

    received = exchanged(payload)
    within = call(
        within_kernel,
        chunks,
        [
            (pre_x, rows(width)),
            (pre_bc, rows(bc_width)),
            (step, rows(LANES)),
            (cumc, rows(LANES)),
            (starts, state_spec),
        ],
        [((tokens, width), f32, rows(width))],
        flops=6 * tokens * CHUNK * width,
        moved=8 << 20,
    )[0]
    incoming, decays = call(
        functools.partial(scan_kernel, parts, ranges),
        1,
        [(received, whole(received.shape))],
        [((STATE, width), f32, whole((STATE, width)))] * 2,
        moved=1 << 20,
    )
    incoming = exchanged(incoming)

    mixed, sums = call(
        mix_kernel,
        chunks,
        [
            (incoming, whole((STATE, width))),
            (pre_x, rows(width)),
            (pre_bc, rows(bc_width)),
            (cumd, rows(LANES)),
            (within, rows(width)),
            (gate_z, rows(width)),
            (d_out, rows(width)),
            (small, small_spec),
            (gain_out, whole((width,))),
        ],
        [((tokens, width), f32, rows(width)), ((parts_head, 2, tokens), f32, pair_line)],
        flops=2 * tokens * STATE * width,
        moved=10 << 20,
    )
    totals = lax.all_to_all(sums, "head", 0, 0)
    normed_out, gate_low, d_mixed, col_out, payload = call(
        functools.partial(gate_kernel, width * parts_head),
        chunks,
        [
            (totals, pair_line),
            (mixed, rows(width)),
            (gate_z, rows(width)),
            (d_out, rows(width)),
            (pre_x, rows(width)),
            (pre_bc, rows(bc_width)),
            (cumd, rows(LANES)),
            (small, small_spec),
            (gain_out, whole((width,))),
        ],
        [
            ((tokens, width), bf16, rows(width)),
            ((tokens, width), bf16, rows(width)),
            ((tokens, width), bf16, rows(width)),
            ((EDGE, width), f32, whole((EDGE, width))),
            ((STATE, width), f32, whole((STATE, width))),
        ],
        flops=2 * tokens * STATE * width,
        moved=14 << 20,
    )

    received = exchanged(payload)
    share = model_width // parts_head
    d_values, d_bc, d_step, d_log, full_starts = call(
        back_kernel,
        chunks,
        [
            (pre_x, rows_back(width)),
            (pre_bc, rows_back(bc_width)),
            (step, rows_back(LANES)),
            (cumc, rows_back(LANES)),
            (cumd, rows_back(LANES)),
            (starts, state_back),
            (incoming, whole((STATE, width))),
            (d_mixed, rows_back(width)),
        ],
        [
            ((tokens, width), f32, rows_back(width)),
            ((tokens, bc_width), f32, rows_back(bc_width)),
            ((tokens, LANES), f32, rows_back(LANES)),
            ((tokens, LANES), f32, rows_back(LANES)),
            ((chunks, STATE, width), f32, state_back),
        ],
        [pltpu.VMEM((STATE, width), f32), pltpu.VMEM((LANES, CHUNK), f32)],
    )
    half_columns = pl.BlockSpec((tokens, half), lambda i: (0, i))
    pair_columns = pl.BlockSpec((tokens, 2 * LANES), lambda i: (0, i))
    grad_z = call(
        product_kernel,
        model_width // half,
        [(normed, half_columns), (gate_low, whole((tokens, width)))],
        [((model_width, width), f32, rows_of(half, width))],
    )[0]
    grad_out = call(
        product_kernel,
        width // (2 * LANES),
        [(normed_out, pair_columns), (cot, whole((tokens, model_width)))],
        [((width, model_width), f32, rows_of(2 * LANES, model_width))],
    )[0]
    received, grad_z, grad_out = lax.optimization_barrier((received, grad_z, grad_out))
    grad_z, grad_out = lax.psum((grad_z, grad_out), ("dp", "seq"))
    later = call(
        functools.partial(scan_back_kernel, parts, ranges),
        1,
        [(received, whole((STATE, width))), (decays, whole((STATE, width)))],
        [((STATE, width), f32, whole((STATE, width)))],
    )[0]
    later = exchanged(later)

    def top(columns):
        return pl.BlockSpec((EDGE, columns), lambda i: (0, 0))

    last_rows = pl.BlockSpec((EDGE, LANES), lambda i: (tokens // EDGE - 1, 0))
    edge_grad = call(
        edge_kernel,
        1,
        [
            (later, whole((STATE, width))),
            (pre_x, top(width)),
            (pre_bc, top(bc_width)),
            (step, top(LANES)),
            (cumd, top(LANES)),
            (cumd, last_rows),
            (d_mixed, pl.BlockSpec((2 * EDGE, width), lambda i: (0, 0))),
            (d_values, top(width)),
            (d_bc, top(bc_width)),
            (small, small_spec),
        ],
        [((EDGE, width + bc_width), f32, whole((EDGE, width + bc_width)))],
    )[0]
    edge_next = from_behind(edge_grad, "seq", -1)

    def rows_before(columns):
        step_rows = CHUNK // EDGE
        return pl.BlockSpec(
            (EDGE, columns),
            lambda i: (jnp.maximum((chunks - 1 - i) * step_rows - 1, 0), 0),
        )

    x_low, own, send, bc_low, bc_rows, step_low, sums = call(
        finish_kernel,
        chunks,
        [
            (core_flag, flag_spec),
            (later, whole((STATE, width))),
            (full_starts, state_back),
            (pre_x, rows_back(width)),
            (pre_bc, rows_back(bc_width)),
            (inner_x, rows_back(width)),
            (inner_bc, rows_back(bc_width)),
            (inner_x, rows_before(width)),
            (inner_bc, rows_before(bc_width)),
            (edge, whole((EDGE, width + bc_width))),
            (edge_next, whole((EDGE, width + bc_width))),
            (step_raw, rows_back(LANES)),
            (step, rows_back(LANES)),
            (cumc, rows_back(LANES)),
            (cumd, rows_back(LANES)),
            (cumd, last_rows),
            (d_mixed, rows_back(width)),
            (d_values, rows_back(width)),
            (d_bc, rows_back(bc_width)),
            (d_step, rows_back(LANES)),
            (d_log, rows_back(LANES)),
            (conv_x, whole(conv_x.shape)),
            (conv_bc, whole(conv_bc.shape)),
            (small, small_spec),
            (col_out, whole((EDGE, width))),
        ],
        [
            ((tokens, width), bf16, rows_back(width)),
            ((tokens, half), bf16, rows_back(half)),
            ((tokens, half), f32, rows_back(half)),
            ((tokens, bc_width), bf16, rows_back(bc_width)),
            (
                (parts_head, bc_share, tokens),
                f32,
                pl.BlockSpec((parts_head, bc_share, CHUNK), lambda i: (0, 0, chunks - 1 - i)),
            ),
            ((tokens, LANES), bf16, rows_back(LANES)),
            ((EDGE, model_width), f32, whole((EDGE, model_width))),
        ],
        [
            pltpu.VMEM((CHUNK + EDGE, width), f32),
            pltpu.VMEM((CHUNK + EDGE, bc_width), f32),
            pltpu.VMEM((CHUNK + EDGE, width), f32),
            pltpu.VMEM((CHUNK + EDGE, bc_width), f32),
        ],
    )
    peer = swap_cores(send)
    blocks = model_width // half
    per = ranges // blocks
    x_rows, small_rows = model_width // ranges, half // ranges
    features = 2 * LANES
    feature_blocks = model_width // features
    by_features = pl.BlockSpec((tokens, features), lambda i: (0, i))
    both, parts_out = call(
        norm_back_kernel,
        feature_blocks,
        [
            (gate_low, whole((tokens, width))),
            (x_low, whole((tokens, width))),
            (bc_low, whole((tokens, bc_width))),
            (step_low, whole((tokens, LANES))),
            (normed_out, whole((tokens, width))),
            (hid, whole((tokens, model_width))),
            (hid, by_features),
            (norm_gain, pl.BlockSpec((features,), lambda i: (i,))),
            (w_z, rows_of(features, width)),
            (w_x, rows_of(features, width)),
            (w_bc, rows_of(features, bc_width)),
            (dt_rows, pl.BlockSpec((heads_here, features), lambda i: (0, i))),
            (w_out, pl.BlockSpec((width, features), lambda i: (0, i))),
            (sums, whole((EDGE, model_width))),
            (bc_rows, whole(bc_rows.shape)),
        ],
        [
            (
                (2, tokens, model_width),
                f32,
                pl.BlockSpec((2, tokens, features), lambda i: (0, 0, i)),
            ),
            (
                (parts_head, bc_share + EDGE, tokens),
                f32,
                whole((parts_head, bc_share + EDGE, tokens)),
            ),
        ],
        [
            pltpu.VMEM((tokens, LANES), f32),
            pltpu.VMEM((tokens, LANES), f32),
            pltpu.VMEM((EDGE, model_width), f32),
        ],
    )
    bc_parts = lax.all_to_all(parts_out, "head", 0, 0)
    shared = pl.BlockSpec((per, x_rows + small_rows, half), lambda i: (i, 0, 0))
    small_block = pl.BlockSpec((ranges, small_rows, half), lambda i: (0, x_rows // small_rows, 0))
    grad_x = call(
        outer_kernel,
        blocks,
        [
            (normed, half_columns),
            (own, whole((tokens, half))),
            (normed_peer, half_columns),
            (peer, whole((tokens, half))),
        ],
        [((ranges, x_rows + small_rows, half), f32, shared)],
    )[0]
    grad_x, bc_parts = lax.optimization_barrier((grad_x, bc_parts))
    grad_x, dots = call(
        share_kernel,
        1,
        [
            (grad_x, pl.BlockSpec(memory_space=pl.ANY)),
            (bc_parts, whole(bc_parts.shape)),
            (step_low, whole(step_low.shape)),
            (normed, whole(normed.shape)),
            (sums, whole(sums.shape)),
        ],
        [
            (grad_x.shape, f32, small_block),
            ((EDGE, tokens), f32, whole((EDGE, tokens))),
        ],
        aliases={0: 0},
    )
    row_dot = dots[6]
    branch_own, norm_own = lax.psum_scatter(both, "head", scatter_dimension=2, tiled=True)
    grad_x = lax.all_to_all(grad_x, "seq", 0, 0)
    lane_block = pl.BlockSpec(grad_x.shape[:2] + (LANES,), lambda i: (0, 0, i))
    grad_x = call(
        total_kernel, half // LANES, [(grad_x, lane_block)], [(grad_x.shape, f32, lane_block)]
    )[0]
    grad_x = lax.all_to_all(grad_x, "seq", 0, 0)
    grad_z = call(
        copy_kernel,
        blocks,
        [(grad_z, rows_of(half, width))],
        [((model_width, width), f32, rows_of(half, width))],
    )[0]
    grad_out = call(
        copy_kernel,
        blocks,
        [(grad_out, rows_of(half // 2, model_width))],
        [((width, model_width), f32, rows_of(half // 2, model_width))],
    )[0]
    branch_own, norm_own, grad_z, grad_out = lax.optimization_barrier(
        (branch_own, norm_own, grad_z, grad_out)
    )
    first = head_pos * share
    rows_own = lax.dynamic_slice_in_dim(hid, first, share, 1).astype(f32)
    output = (rows_own + branch_own).astype(bf16)[None]
    rows_all = hid.astype(f32)
    scale_in = lax.rsqrt(jnp.mean(rows_all * rows_all, axis=1, keepdims=True) + epsilon)
    gain_own = lax.dynamic_slice_in_dim(norm_gain, first, share, 0)
    cot_own = lax.dynamic_slice_in_dim(cot, first, share, 1).astype(f32)
    unit_own = rows_own * scale_in
    grad_in = scale_in * (norm_own * gain_own - unit_own * row_dot[:, None] / model_width)
    hidden_grad = (cot_own + grad_in).astype(bf16)[None]
    grad_x, grad_z, grad_out, output, hidden_grad = lax.optimization_barrier(
        (grad_x, grad_z, grad_out, output, hidden_grad)
    )
    x_peer = swap_cores(grad_x)
    grads = grad_x
    grad_x = call(
        join_kernel,
        blocks,
        [(core_flag, flag_spec), (grads, shared), (x_peer, shared)],
        [((model_width, width), f32, rows_of(half, width))],
    )[0]
    taps = conv_x.shape[0]
    shapes = [
        (bc_share, model_width),
        (heads_here, model_width),
        (taps, width),
        (taps, bc_width),
        (width,),
        (bc_width,),
        (width,),
        (share,),
        (EDGE, LANES),
    ]
    dealt = call(
        deal_kernel,
        1,
        [
            (grads, small_block),
            (x_peer, small_block),
        ],
        [(shape, f32, whole(shape)) for shape in shapes],
        [pltpu.VMEM((EDGE, model_width), f32)],
    )
    g_bc, g_dt, g_conv_x, g_conv_bc, g_bias_x, g_bias_bc, g_gain, g_norm, by_head = dealt
    return (
        output,
        hidden_grad,
        g_norm,
        grad_z,
        grad_x,
        g_bc.T,
        g_dt.T,
        g_conv_x,
        g_conv_bc,
        g_bias_x,
        g_bias_bc,
        by_head[1, :heads_here],
        by_head[0, :heads_here],
        by_head[2, :heads_here],
        g_gain,
        grad_out,
    )


def solution(mesh):
    placed = (
        P("dp", "seq", None),
        P("dp", "seq", None),
        P(),
        P(None, "head"),
        P(None, "head"),
        P(),
        P(None, "head"),
        P(None, "head"),
        P(),
        P("head"),
        P(),
        P("head"),
        P("head"),
        P("head"),
        P("head"),
        P("head", None),
    )
    return jax.shard_map(
        per_device,
        mesh=mesh,
        in_specs=placed,
        out_specs=(
            P("dp", "seq", "head"),
            P("dp", "seq", "head"),
            P("head"),
            P(None, "head"),
            P(None, "head"),
            P(None, "head"),
            P(None, "head"),
            P(None, "head"),
            P(),
            P("head"),
            P(),
            P("head"),
            P("head"),
            P("head"),
            P("head"),
            P("head", None),
        ),
        check_vma=False,
    )
```

time: 1090 us -> 314 us (0.29); the launches traced: 1070 us -> 311 us
  waiting for transfers between devices: 356 us -> 56.6 us
  local copies, waits for them, and re-layouts: 190 us -> 9.4 us
  other arithmetic: 128 us -> 4.8 us
  matrix products: 126 us -> 8.53 us
  Pallas kernels: 0 us -> 111 us
  blocking collectives: 153 us -> 57.3 us
  starting transfers between devices: 105 us -> 48.3 us
    ppermute x32 -> x2, waiting for transfers between devices: 261 us -> 4.7 us  [from_behind(): return lax.ppermute(shard, axis, pairs)]
    psum x4 -> x0, blocking collectives: 153 us -> none  [the longest x1 131 us: per_device(): lax.psum((grad_norm_gain, grad_w_z, grad_w_x, grad_w_bc, grad_w_dt, grad_...]
    dot_general x46 -> x2, matrix products: 126 us -> 8.53 us  [the longest x1 4.31 us: per_device(): gate_z = jnp.dot(normed, w_z, preferred_element_type=f32)]
    pallas_call x0 -> x20, Pallas kernels: none -> 111 us  [call(): pl.pallas_call(kernel, grid=(grid,), in_specs=[spec for _, spec in ins],...]
    ppermute x32 -> x2, starting transfers between devices: 105 us -> 5.97 us  [from_behind(): return lax.ppermute(shard, axis, pairs)]
    dynamic_update_slice x12 -> x0, local copies, waits for them, and re-layouts: 72.9 us -> none  [ssd_outputs(): lax.scan(jax.checkpoint(block_step), start_state, (split_rows(values), sp...]
    all_to_all x0 -> x2, blocking collectives: none -> 57.3 us  [the longest x1 48.7 us: per_device(): grad_x = lax.all_to_all(grad_x, 'seq', 0, 0)]
    reduce_scatter x2 -> x1, waiting for transfers between devices: 45.2 us -> 0.01 us  [per_device(): lax.psum_scatter(both, 'head', scatter_dimension=2, tiled=True)]
  transfers between devices with their start and end apart: 36 -> 13, of which waited for: 35 -> 7; matrix products, arithmetic and copies ran while one was open for 8% -> 5% of each run, Pallas kernels for 0% -> 24%
where the time goes in v1:
time: 314 us; the launch traced here: 311 us
  Pallas kernels  111 us (35%)
  blocking collectives  57.3 us (18%)
  waiting for transfers between devices  56.6 us (18%)
  starting transfers between devices  48.3 us (15%)
  between operations  15.7 us (5%)
  local copies, waits for them, and re-layouts  9.4 us (3%)
  matrix products  8.53 us (3%)
  other arithmetic  4.8 us (2%)
    pallas_call x20, Pallas kernels, call(): pl.pallas_call(kernel, grid=(grid,), in_specs=[spec for _, spec in ins],...  111 us
    all_to_all x1, blocking collectives, per_device(): grad_x = lax.all_to_all(grad_x, 'seq', 0, 0)  48.7 us
    psum x1, waiting for transfers between devices, per_device(): grad_z, grad_out = lax.psum((grad_z, grad_out), ('dp', 'seq'))  39.1 us
    all_to_all x4, starting transfers between devices, exchanged(): return lax.all_to_all(blocks, 'seq', 0, 0).reshape(array.shape)  24.5 us
    all_to_all x1, blocking collectives, per_device(): totals = lax.all_to_all(sums, 'head', 0, 0)  8.51 us
    ppermute x3, waiting for transfers between devices, swap_cores(): return lax.ppermute(shard, 'dp', [(0, 1), (1, 0)])  7.85 us
    all_to_all x1, starting transfers between devices, per_device(): grad_x = lax.all_to_all(grad_x, 'seq', 0, 0)  7.02 us
    ppermute x3, starting transfers between devices, swap_cores(): return lax.ppermute(shard, 'dp', [(0, 1), (1, 0)])  6.6 us
  transfers between devices with their start and end apart: 13, of which 7 were waited for; matrix products, arithmetic and copies ran while one was open for 5% of the time, Pallas kernels for 24%

profile of v1, /device:TPU:1, one launch (start us, length us, event | category | flops | bytes accessed | tf_op | source)
XLA Modules:
  0.0 311.3 jit_solution(9022744206375744194)
XLA Ops:
  8.0 6.3 %shard_map.279 = (bf16[512,1536]{1,0:T(8,128)(2,1)}, f32[512,1536]{1,0:T(8,128)}, f32[512,768]{1,0:T(8,128)}, f32[512,256]{1,0:T(8,128)}, f32[512,128]{1,0:T(8,128)}, /*index=5*/f32[8,1024]{1,0:T(8,128)}) custom-call(bf16[512,1536]{1,0:T(8,128)(2,1)} %bitcast.45, f32[1536]{0:T(1024)} %gain.7, bf16[1536,768]{1,0:T(8,128)(2,1)} %wx.3, bf16[1536,256]{1,0:T(8,128)(2,1)} %wbc.3, ...), custom_call_target="tpu_custom_call" | custom-call | flops 1610612736 | bytes 18874368 | tf_op jit(solution)/shard_map/pallas_call | solution.py:623
  14.3 4.5 %collective-permute-start = (f32[8,1024]{1,0:T(8,128)}, f32[8,1024]{1,0:T(8,128)S(1)}, u32[]{:S(2)}, u32[]{:S(2)}) collective-permute-start(f32[8,1024]{1,0:T(8,128)} %get-tuple-element.78), channel_id=1, source_target_pairs={{0,4},{4,8},{8,12},{12,16},{16,20},{20,24},{24,28},{28,32},{32,36}... | collective-permute-start | bytes 98312 | tf_op jit(solution)/shard_map/ppermute | solution.py:641
  20.8 6.9 %shard_map.280 = (f32[512,768]{1,0:T(8,128)}, f32[512,256]{1,0:T(8,128)}, f32[512,128]{1,0:T(8,128)}, f32[512,128]{1,0:T(8,128)}, f32[512,128]{1,0:T(8,128)}, /*...) custom-call(f32[8,1024]{1,0:T(8,128)} %copy-done.7, f32[512,768]{1,0:T(8,128)} %get-tuple-element.79.inx.before_x, ...), custom_call_target="tpu_custom_call" | custom-call | flops 100663296 | bytes 8388608 | tf_op jit(solution)/shard_map/pallas_call | solution.py:623
  27.7 7.6 %all-to-all-start = ((f32[16,8,896]{2,1,0:T(8,128)}), f32[16,8,896]{2,1,0:T(8,128)}, u32[]{:S(2)}, u32[]{:S(2)}) async-start(f32[16,8,896]{2,1,0:T(8,128)} %bitcast.55), calls=%async_computation | async-start | bytes 917504 | tf_op jit(solution)/shard_map/all_to_all | solution.py:761
  54.1 5.5 %shard_map.282.within = f32[512,768]{1,0:T(8,128)} custom-call(f32[512,768]{1,0:T(8,128)} %get-tuple-element.84.prex, f32[512,256]{1,0:T(8,128)} %get-tuple-element.85.prebc, f32[512,128]{1,0:T(8,128)} %get-tuple-element.87.step_in, f32[512,128]{1,0:T(8,128)} %get-tuple-element.88.cumc_in, f32[4,128,768]{2,1,0:T(8,128)} %get-tuple-element.89.starts), custom_call_target="tpu_custom_call" | custom-call | flops 301989888 | bytes 8388608 | tf_op jit(solution)/shard_map/pallas_call | solution.py:623
  60.3 5.9 %shard_map.283 = (f32[512,768]{1,0:T(8,128)}, f32[4,2,512]{2,1,0:T(2,128)}) custom-call(f32[128,768]{1,0:T(8,128)} %bitcast.48, f32[512,768]{1,0:T(8,128)} %get-tuple-element.84.prex, f32[512,256]{1,0:T(8,128)} %get-tuple-element.85.prebc, f32[512,128]{1,0:T(8,128)} %get-tuple-element.86.cumd.total.cumd_in, f32[512,768]{1,0:T(8,128)} %shard_map.282.within, ...), custom_call_target="tpu_custom_call" | custom-call | flops 100663296 | bytes 10485760 | tf_op jit(solution)/shard_map/pallas_call | solution.py:623
  66.2 8.5 %all_to_all.40.totals = f32[4,2,512]{2,1,0:T(2,128)} all-to-all(f32[4,2,512]{2,1,0:T(2,128)} %get-tuple-element.90), channel_id=1, replica_groups=mesh['dp'=2,'seq'=16,'head'=4] {'head'}, dimensions={0} | all-to-all | bytes 32768 | tf_op jit(solution)/shard_map/all_to_all | solution.py:805
  74.7 6.2 %shard_map.284 = (bf16[512,768]{1,0:T(8,128)(2,1)}, bf16[512,768]{1,0:T(8,128)(2,1)}, bf16[512,768]{1,0:T(8,128)(2,1)}, f32[8,768]{1,0:T(8,128)}, f32[128,768]{1,0:T(8,128)}) custom-call(f32[4,2,512]{2,1,0:T(2,128)} %all_to_all.40.totals, f32[512,768]{1,0:T(8,128)} %get-tuple-element.91.mixed_in, f32[512,768]{1,0:T(8,128)} %fusion.11.gate_z, ...), custom_call_target="tpu_custom_call" | custom-call | flops 100663296 | bytes 14680064 | tf_op jit(solution)/shard_map/pallas_call | solution.py:623
  81.0 6.6 %all-to-all-start.3 = ((f32[16,8,768]{2,1,0:T(8,128)}), f32[16,8,768]{2,1,0:T(8,128)S(1)}, u32[]{:S(2)}, u32[]{:S(2)}) async-start(f32[16,8,768]{2,1,0:T(8,128)} %bitcast.56), calls=%async_computation.3 | async-start | bytes 786432 | tf_op jit(solution)/shard_map/all_to_all | solution.py:761
  87.6 5.4 %shard_map.285 = f32[1536,768]{1,0:T(8,128)} custom-call(bf16[512,1536]{1,0:T(8,128)(2,1)} %get-tuple-element.77.left.normed, bf16[512,768]{1,0:T(8,128)(2,1)} %get-tuple-element.93.right.dg), custom_call_target="tpu_custom_call" | custom-call | tf_op jit(solution)/shard_map/pallas_call | solution.py:623
  93.0 5.0 %shard_map.286 = f32[768,1536]{1,0:T(8,128)} custom-call(bf16[512,768]{1,0:T(8,128)(2,1)} %get-tuple-element.94.left.ahead, bf16[512,1536]{1,0:T(8,128)(2,1)} %bitcast.52), custom_call_target="tpu_custom_call" | custom-call | tf_op jit(solution)/shard_map/pallas_call | solution.py:623
  100.6 6.7 %all-to-all-start.4 = ((f32[16,8,768]{2,1,0:T(8,128)}), f32[16,8,768]{2,1,0:T(8,128)S(1)}, u32[]{:S(2)}, u32[]{:S(2)}) async-start(f32[16,8,768]{2,1,0:T(8,128)} %bitcast.54), calls=%async_computation.4 | async-start | bytes 786432 | tf_op jit(solution)/shard_map/all_to_all | solution.py:761
  107.3 10.3 %shard_map.288 = (f32[512,768]{1,0:T(8,128)}, f32[512,256]{1,0:T(8,128)}, f32[512,128]{1,0:T(8,128)}, f32[512,128]{1,0:T(8,128)}, f32[4,128,768]{2,1,0:T(8,128)}) custom-call(f32[512,768]{1,0:T(8,128)} %get-tuple-element.84.prex, f32[512,256]{1,0:T(8,128)} %get-tuple-element.85.prebc, f32[512,128]{1,0:T(8,128)} %get-tuple-element.87.step_in, ...), custom_call_target="tpu_custom_call" | custom-call | tf_op jit(solution)/shard_map/pallas_call | solution.py:623
  126.4 9.0 %shard_map.290 = (bf16[512,768]{1,0:T(8,128)(2,1)}, bf16[512,384]{1,0:T(8,128)(2,1)}, f32[512,384]{1,0:T(8,128)}, bf16[512,256]{1,0:T(8,128)(2,1)}, f32[4,64,512...) custom-call(s32[1]{0:T(128)} %bitcast.2.core, f32[128,768]{1,0:T(8,128)} %bitcast.51, ...), custom_call_target="tpu_custom_call" | custom-call | tf_op jit(solution)/shard_map/pallas_call | solution.py:623
  135.5 12.9 %shard_map.292 = (f32[2,512,1536]{2,1,0:T(8,128)}, f32[4,72,512]{2,1,0:T(8,128)}) custom-call(bf16[512,768]{1,0:T(8,128)(2,1)} %get-tuple-element.93.right.dg, bf16[512,768]{1,0:T(8,128)(2,1)} %get-tuple-element.107.dx, bf16[512,256]{1,0:T(8,128)(2,1)} %get-tuple-element.108.dbc, bf16[512,128]{1,0:T(8,128)(2,1)} %get-tuple-element.109.dst.step_low, ...), custom_call_target="tpu_custom_call" | custom-call | tf_op jit(solution)/shard_map/pallas_call | solution.py:623
  148.3 6.4 %collective-permute-start.2 = (f32[512,1536]{1,0:T(8,128)}, f32[512,1536]{1,0:T(8,128)S(1)}, u32[]{:S(2)}, u32[]{:S(2)}) collective-permute-start(f32[512,1536]{1,0:T(8,128)} %get-tuple-element.105), channel_id=1, source_target_pairs={{0,64},{64,0},{1,65},{65,1},{2,66},{66,2},{3,67},{67,3},{4,68},{68... | collective-permute-start | bytes 9437192 | tf_op jit(solution)/shard_map/ppermute | solution.py:645
  163.1 6.4 %shard_map.291.buffer = f32[16,120,384]{2,1,0:T(8,128)} custom-call(bf16[512,1536]{1,0:T(8,128)(2,1)} %get-tuple-element.77.left.normed, bf16[512,384]{1,0:T(8,128)(2,1)} %get-tuple-element.104.right, f32[512,1536]{1,0:T(8,128)} %copy-done.4, f32[512,384]{1,0:T(8,128)} %collective-permute-done.3.right_peer), custom_call_target="tpu_custom_call" | custom-call | tf_op jit(solution)/shard_map/pallas_call | solution.py:623
  173.1 48.7 %all_to_all.41.parts = f32[16,120,384]{2,1,0:T(8,128)} all-to-all(f32[16,120,384]{2,1,0:T(8,128)} %get-tuple-element.115), channel_id=1, replica_groups=mesh['dp'=2,'seq'=16,'head'=4] {'seq'}, dimensions={0} | all-to-all | bytes 5898240 | tf_op jit(solution)/shard_map/all_to_all | solution.py:1037
  226.3 7.0 %all-to-all-start.7 = ((f32[16,120,384]{2,1,0:T(8,128)}), f32[16,120,384]{2,1,0:T(8,128)S(1)}, u32[]{:S(2)}, u32[]{:S(2)}) async-start(f32[16,120,384]{2,1,0:T(8,128)} %shard_map.294), calls=%async_computation.7 | async-start | bytes 5898240 | tf_op jit(solution)/shard_map/all_to_all | solution.py:1042
  236.6 39.1 %all-reduce.4.cloned.1.call-done = (f32[1536,768]{1,0:T(8,128)}, f32[768,1536]{1,0:T(8,128)}) async-done(((f32[1536,768]{1,0:T(8,128)}, f32[768,1536]{1,0:T(8,128)}), (f32[1536,768]{1,0:T(8,128)}, f32[768,1536]{1,0:T(8,128)})) %all-reduce.4.cloned.1.call-update) | async-done | bytes 9437200 | tf_op jit(solution)/shard_map/psum | solution.py:870
  275.7 5.0 %shard_map.295 = f32[1536,768]{1,0:T(8,128)} custom-call(f32[1536,768]{1,0:T(8,128)} %get-tuple-element.138.source), custom_call_target="tpu_custom_call" | custom-call | tf_op jit(solution)/shard_map/pallas_call | solution.py:623
  280.8 5.0 %shard_map.296 = f32[768,1536]{1,0:T(8,128)} custom-call(f32[768,1536]{1,0:T(8,128)} %get-tuple-element.139.source), custom_call_target="tpu_custom_call" | custom-call | tf_op jit(solution)/shard_map/pallas_call | solution.py:623
  289.7 5.5 %collective-permute-done.4.theirs = f32[16,120,384]{2,1,0:T(8,128)} collective-permute-done((f32[16,120,384]{2,1,0:T(8,128)S(1)}, f32[16,120,384]{2,1,0:T(8,128)}, u32[]{:S(2)}, u32[]{:S(2)}) %collective-permute-start.4) | collective-permute-done | bytes 2949152 | tf_op jit(solution)/shard_map/ppermute | solution.py:645
  298.6 5.2 %shard_map.298 = f32[1536,768]{1,0:T(8,128)} custom-call(s32[1]{0:T(128)} %bitcast.2.core, f32[16,120,384]{2,1,0:T(8,128)} %copy-done, f32[16,120,384]{2,1,0:T(8,128)} %collective-permute-done.4.theirs), custom_call_target="tpu_custom_call" | custom-call | tf_op jit(solution)/shard_map/pallas_call | solution.py:623
  (60 shorter events, 59.9 us)
Async XLA Ops:
  8.0 10.8 %copy-start.9 = (f32[12]{0:T(128)S(1)}, f32[12]{0:T(128)}, u32[]{:S(2)}) copy-start(f32[12]{0:T(128)} %param.29) | copy-start | bytes 148
  8.0 10.8 %copy-start.10 = (f32[12]{0:T(128)S(1)}, f32[12]{0:T(128)}, u32[]{:S(2)}) copy-start(f32[12]{0:T(128)} %param.28) | copy-start | bytes 148
  8.0 10.8 %copy-start.11 = (f32[12]{0:T(128)S(1)}, f32[12]{0:T(128)}, u32[]{:S(2)}) copy-start(f32[12]{0:T(128)} %param.27) | copy-start | bytes 148
  14.3 21.0 %copy-start.1 = (bf16[512,1536]{1,0:T(8,128)(2,1)S(1)}, bf16[512,1536]{1,0:T(8,128)(2,1)}, u32[]{:S(2)}) copy-start(bf16[512,1536]{1,0:T(8,128)(2,1)} %get-tuple-element.77.left.normed) | copy-start | bytes 4718596
  14.3 5.8 %collective-permute-start = (f32[8,1024]{1,0:T(8,128)}, f32[8,1024]{1,0:T(8,128)S(1)}, u32[]{:S(2)}, u32[]{:S(2)}) collective-permute-start(f32[8,1024]{1,0:T(8,128)} %get-tuple-element.78), channel_id=1, source_target_pairs={{0,4},{4,8},{8,12},{12,16},{16,20},{20,24},{24,28},{28,32},{32,36}... | collective-permute-start | bytes 98312 | tf_op jit(solution)/shard_map/ppermute | solution.py:641
  20.2 0.6 copy-start.7
  27.7 16.5 %all-to-all-start = ((f32[16,8,896]{2,1,0:T(8,128)}), f32[16,8,896]{2,1,0:T(8,128)}, u32[]{:S(2)}, u32[]{:S(2)}) async-start(f32[16,8,896]{2,1,0:T(8,128)} %bitcast.55), calls=%async_computation | async-start | bytes 917504 | tf_op jit(solution)/shard_map/all_to_all | solution.py:761
  35.3 14.5 %copy-start.5 = (bf16[1,512,1536]{2,1,0:T(8,128)(2,1)S(1)}, bf16[1,512,1536]{2,1,0:T(8,128)(2,1)}, u32[]{:S(2)}) copy-start(bf16[1,512,1536]{2,1,0:T(8,128)(2,1)} %param.17) | copy-start | bytes 4718596
  46.3 13.3 %all-to-all-start.1 = ((f32[16,8,768]{2,1,0:T(8,128)}), f32[16,8,768]{2,1,0:T(8,128)S(1)}, u32[]{:S(2)}, u32[]{:S(2)}) async-start(f32[16,8,768]{2,1,0:T(8,128)} %bitcast.57), calls=%async_computation.1 | async-start | bytes 786432 | tf_op jit(solution)/shard_map/all_to_all | solution.py:761
  59.5 0.7 copy-start.2
  81.0 17.0 %all-to-all-start.3 = ((f32[16,8,768]{2,1,0:T(8,128)}), f32[16,8,768]{2,1,0:T(8,128)S(1)}, u32[]{:S(2)}, u32[]{:S(2)}) async-start(f32[16,8,768]{2,1,0:T(8,128)} %bitcast.56), calls=%async_computation.3 | async-start | bytes 786432 | tf_op jit(solution)/shard_map/all_to_all | solution.py:761
  87.6 188.2 %all-reduce.4.cloned.1.call-start = ((), (), s32[]{:S(2)}) async-start(), calls=%async_computation.10 | async-start | bytes 18874368 | tf_op jit(solution)/shard_map/psum | solution.py:870
  98.0 0.7 copy-start.6
  100.6 17.0 %all-to-all-start.4 = ((f32[16,8,768]{2,1,0:T(8,128)}), f32[16,8,768]{2,1,0:T(8,128)S(1)}, u32[]{:S(2)}, u32[]{:S(2)}) async-start(f32[16,8,768]{2,1,0:T(8,128)} %bitcast.54), calls=%async_computation.4 | async-start | bytes 786432 | tf_op jit(solution)/shard_map/all_to_all | solution.py:761
  107.3 178.5 %reduce-scatter.2.cloned.1.call-start = ((), (), s32[]{:S(2)}) async-start(), calls=%async_computation.9 | async-start | bytes 7864320 | tf_op jit(solution)/shard_map/reduce_scatter | solution.py:1036
  117.6 0.7 copy-start.3
  120.3 5.5 %collective-permute-start.1 = (f32[8,1024]{1,0:T(8,128)}, f32[8,1024]{1,0:T(8,128)S(1)}, u32[]{:S(2)}, u32[]{:S(2)}) collective-permute-start(f32[8,1024]{1,0:T(8,128)} %shard_map.289), channel_id=1, source_target_pairs={{4,0},{8,4},{12,8},{16,12},{20,16},{24,20},{28,24},{32,28},{36,32}... | collective-permute-start | bytes 98312 | tf_op jit(solution)/shard_map/ppermute | solution.py:641
  148.3 13.1 %collective-permute-start.2 = (f32[512,1536]{1,0:T(8,128)}, f32[512,1536]{1,0:T(8,128)S(1)}, u32[]{:S(2)}, u32[]{:S(2)}) collective-permute-start(f32[512,1536]{1,0:T(8,128)} %get-tuple-element.105), channel_id=1, source_target_pairs={{0,64},{64,0},{1,65},{65,1},{2,66},{66,2},{3,67},{67,3},{4,68},{68... | collective-permute-start | bytes 9437192 | tf_op jit(solution)/shard_map/ppermute | solution.py:645
  154.8 6.6 %collective-permute-start.3 = (f32[512,384]{1,0:T(8,128)}, f32[512,384]{1,0:T(8,128)}, u32[]{:S(2)}, u32[]{:S(2)}) collective-permute-start(f32[512,384]{1,0:T(8,128)} %get-tuple-element.106), channel_id=1, source_target_pairs={{0,64},{64,0},{1,65},{65,1},{2,66},{66,2},{3,67},{67,3},{4,68},{68... | collective-permute-start | bytes 2359304 | tf_op jit(solution)/shard_map/ppermute | solution.py:645
  154.9 15.0 %all-to-all-start.5 = ((f32[4,72,512]{2,1,0:T(8,128)}), f32[4,72,512]{2,1,0:T(8,128)}, u32[]{:S(2)}, u32[]{:S(2)}) async-start(f32[4,72,512]{2,1,0:T(8,128)} %get-tuple-element.112), calls=%async_computation.5 | async-start | bytes 1179648 | tf_op jit(solution)/shard_map/all_to_all | solution.py:1004
  161.4 1.7 copy-start.4
  226.3 63.4 %all-to-all-start.7 = ((f32[16,120,384]{2,1,0:T(8,128)}), f32[16,120,384]{2,1,0:T(8,128)S(1)}, u32[]{:S(2)}, u32[]{:S(2)}) async-start(f32[16,120,384]{2,1,0:T(8,128)} %shard_map.294), calls=%async_computation.7 | async-start | bytes 5898240 | tf_op jit(solution)/shard_map/all_to_all | solution.py:1042
  289.6 5.6 %copy-start = (f32[16,120,384]{2,1,0:T(8,128)}, f32[16,120,384]{2,1,0:T(8,128)S(1)}, u32[]{:S(2)}) copy-start(f32[16,120,384]{2,1,0:T(8,128)S(1)} %all-to-all-done.7.mine) | copy-start | bytes 8847364
  289.6 5.6 %collective-permute-start.4 = (f32[16,120,384]{2,1,0:T(8,128)S(1)}, f32[16,120,384]{2,1,0:T(8,128)}, u32[]{:S(2)}, u32[]{:S(2)}) collective-permute-start(f32[16,120,384]{2,1,0:T(8,128)S(1)} %all-to-all-done.7.mine), channel_id=1, source_target_pairs={{0,64},{64,0},{1,65},{65,1},{2,66},{66,2},{3,67},{67,3},{4,68},{68... | collective-permute-start | bytes 8847368 | tf_op jit(solution)/shard_map/ppermute | solution.py:645
  (1 other events, 0.6 us)
Sparse Core Ops, SparseCore 0:
  98.1 177.5 all-reduce.3
Sparse Core Ops, SparseCore 1:
  148.4 73.4 reduce-scatter.1

commit v2 on v1

--- a/solution.py
+++ b/solution.py
@@ -41,6 +41,11 @@
         terms.append(term)
         value = value - term.astype(f32)
     return terms
+
+
+def dot_split(left, right):
+    high, rest = parts_of(right, 2)
+    return dot(left, high) + dot(left, rest)
 
 
 def head_map(width):
@@ -169,7 +174,7 @@
     heads = head_map(width)
     weights = spread(jnp.exp(last - cumc) * step, heads)
     keep = spread(jnp.exp(jnp.broadcast_to(last, (EDGE, LANES))), heads)[0:1, :]
-    state[...] = keep * state[...] + dot(low(keys_t), low(values * weights))
+    state[...] = keep * state[...] + dot_split(low(keys_t), values * weights)
     base[...] = base[...] + last
 
     @pl.when(i == pl.num_programs(0) - 1)
@@ -196,55 +201,54 @@
         carry = decays[here, :] * carry + received[here, :]
 
 
-def within_kernel(prex, prebc, step_in, cumc_in, starts, out):
+def within_kernel(prex, prebc, step_in, cumc_in, starts, small, out):
     width = prex.shape[1]
     heads = head_map(width)
-    values = low(silu(prex[...])).astype(f32)
+    act_x = silu(prex[...])
+    values = low(act_x).astype(f32)
     act_bc = low(silu(prebc[...]))
     keys, reads = act_bc[:, :STATE], act_bc[:, STATE:]
     step, cumc = step_in[...], cumc_in[...]
-    cum_t = jnp.transpose(cumc)
-    scaled = values * spread(step, heads)
-    carried = spread(jnp.exp(cumc), heads) * dot(reads, low(starts[0]))
+    cum_t, step_t = jnp.transpose(cumc), jnp.transpose(step)
+    carried = spread(jnp.exp(cumc), heads) * dot_split(reads, starts[0])
+    carried = carried + spread(small[...], heads)[2:3, :] * act_x
     scores = dot_nt(reads, keys)
     row, column = row_col()
     causal = row >= column
     first = lax.broadcasted_iota(jnp.int32, (CHUNK, LANES), 1) < HEADDIM
     for pair in range(width // LANES):
         lanes = slice(pair * LANES, (pair + 1) * LANES)
-        pieces = []
+        pieces, rests = [], []
         for h in (2 * pair, 2 * pair + 1):
             decayed = exp_below(causal, cumc[:, h : h + 1] - cum_t[h : h + 1, :])
-            pieces.append(low(decayed * scores))
-        here = scaled[:, lanes]
-        stacked = jnp.concatenate(
-            [low(jnp.where(first, here, 0.0)), low(jnp.where(first, 0.0, here))], axis=0
-        )
-        out[:, lanes] = carried[:, lanes] + dot(jnp.concatenate(pieces, axis=1), stacked)
-
-
-def mix_kernel(incoming, prex, prebc, cumd, within, gate_z, d_out, small, gain, mixed_out, sums):
-    width = prex.shape[1]
-    heads = head_map(width)
-    reads = low(silu(prebc[:, STATE:]))
-    ssd = within[...] + spread(jnp.exp(cumd[...]), heads) * dot(reads, low(incoming[...]))
-    skip = spread(small[...], heads)[2:3, :]
-    mixed = ssd + skip * silu(prex[...])
+            high, rest = parts_of(decayed * scores * step_t[h : h + 1, :], 2)
+            pieces.append(high)
+            rests.append(rest)
+        here = values[:, lanes]
+        halves = [low(jnp.where(first, here, 0.0)), low(jnp.where(first, 0.0, here))]
+        mixing = jnp.concatenate(pieces + rests, axis=1)
+        out[:, lanes] = carried[:, lanes] + dot(mixing, jnp.concatenate(halves * 2, axis=0))
+
+
+def mix_kernel(incoming, pre_reads, cumd, within, gate_z, d_out, gain, mixed_out, sums):
+    heads = head_map(within.shape[1])
+    reads = low(silu(pre_reads[...]))
+    mixed = within[...] + spread(jnp.exp(cumd[...]), heads) * dot_split(reads, incoming[...])
     mixed_out[...] = mixed
     gated = mixed * silu(gate_z[...])
     squares = row_sum(gated * gated)
     products = row_sum(d_out[...] * as_row(gain) * gated)
     column = lax.broadcasted_iota(jnp.int32, (CHUNK, LANES), 1)
     both = jnp.where(column == 0, squares, jnp.where(column == 1, products, 0.0))
-    sums[...] = jnp.broadcast_to(jnp.transpose(both)[0:2, :][None], sums.shape)
+    sums[...] = jnp.transpose(both)[0:2, :]
 
 
 def gate_kernel(
-    inner_all, totals, mixed_in, gate_z, d_out, prex, prebc, cumd, small, gain,
+    inner_all, totals, second, third, fourth, mixed_in, gate_z, d_out, pre_reads, cumd, gain,
     normed_out, gate_low, d_mixed, col_out, payload,
 ):
     i = pl.program_id(0)
-    width = prex.shape[1]
+    width = mixed_in.shape[1]
     heads = head_map(width)
 
     @pl.when(i == 0)
@@ -252,9 +256,7 @@
         col_out[...] = jnp.zeros(col_out.shape, f32)
         payload[...] = jnp.zeros(payload.shape, f32)
 
-    all_sums = totals[0]
-    for k in range(1, totals.shape[0]):
-        all_sums = all_sums + totals[k]
+    all_sums = (totals[...] + second[...]) + (third[...] + fourth[...])
     squares, products = (
         jnp.transpose(jnp.broadcast_to(all_sums[r : r + 1, :], (CHUNK, CHUNK)))[:, 0:1]
         for r in range(2)
@@ -278,14 +280,13 @@
     gate_low[...] = gate_grad
     g = g_low.astype(f32)
     col_out[0:1, :] += column_sum(d_normed * unit)
-    col_out[1:2, :] += column_sum(g * silu(prex[...]))
-    reads_t = jnp.transpose(low(silu(prebc[:, STATE:])).astype(f32))
-    payload[...] += dot(low(reads_t), low(g * spread(jnp.exp(cumd[...]), heads)))
+    reads_t = jnp.transpose(low(silu(pre_reads[...])).astype(f32))
+    payload[...] += dot_split(low(reads_t), g * spread(jnp.exp(cumd[...]), heads))
 
 
 def back_kernel(
     prex, prebc, step_in, cumc_in, cumd, starts, incoming, d_mixed,
-    d_values, d_bc, d_step, d_log, full_starts,
+    d_values, d_bc, d_step, d_log,
     later, gy_t,
 ):
     i = pl.program_id(0)
@@ -310,15 +311,14 @@
     )
     tops = spread(jnp.exp(tops), heads)
     start = starts[0] + tops[0:1, :] * incoming[...]
-    full_starts[0] = start
     keep = tops[EDGE : EDGE + 1, :]
-    start_low = low(start)
+    start_low, start_rest = parts_of(start, 2)
     step_wide = spread(step, heads)
     out_wide = spread(jnp.exp(last - cumc), heads)
     g_low = d_mixed[...]
     g = g_low.astype(f32)
     g_in = g * spread(jnp.exp(cumc), heads)
-    g_in_low = low(g_in)
+    g_in_low, g_in_rest = parts_of(g_in, 2)
 
     row, column = row_col()
     causal = row <= column
@@ -348,9 +348,11 @@
 
     d_keys = dot(low(d_scores_t), reads) + dot_nt(low(values * step_wide * out_wide), later_low)
     d_reads = dot(low(jnp.transpose(d_scores_t)), keys) + dot_nt(g_in_low, start_low)
+    d_reads = d_reads + dot_nt(g_in_low, start_rest) + dot_nt(g_in_rest, start_low)
     d_bc[:, :STATE] = d_keys
     d_bc[:, STATE:] = d_reads
-    from_start = per_head_sum(g_in * dot(reads, start_low), heads)
+    from_start = dot(reads, start_low) + dot(reads, start_rest)
+    from_start = per_head_sum(g_in * from_start, heads)
     step_onward = per_head_sum(values * onward, heads)
     d_step[...] = step_within + step_onward
     across = column_sum(start * later[...])
@@ -396,7 +398,7 @@
 
 
 def finish_kernel(
-    core, incoming, full_starts, prex, prebc, inx, inbc, before_x, before_bc, edge, edge_next,
+    core, incoming, starts, early, prex, prebc, inx, inbc, before_x, before_bc, edge, edge_next,
     sraw, step_in, cumc_in, cumd_in, total, d_mixed, d_values, d_bc, d_step, d_log, cx, cbc, small,
     col_in,
     x_low, own, send, bc_low, bc_rows, step_out, sums,
@@ -413,7 +415,7 @@
         ext_x[CHUNK:, :] = edge_next[:, :width]
         ext_bc[CHUNK:, :] = edge_next[:, width:]
         sums[...] = jnp.zeros(sums.shape, f32)
-        sums[5:7, :width] = col_in[0:2, :]
+        sums[5:6, :width] = col_in[0:1, :]
 
     late = incoming[...]
     late_low = low(late)
@@ -433,7 +435,8 @@
     d_keys = d_bc[:, :STATE] + dot_nt(low(values * step_wide * out_wide), late_low)
     step_onward = per_head_sum(values * onward, heads)
     before = cumd[CHUNK - 1 : CHUNK, :] - cumc_in[CHUNK - 1 : CHUNK, :]
-    across = column_sum(full_starts[0] * late)
+    tops = spread(jnp.exp(jnp.broadcast_to(before, (EDGE, LANES))), heads)[0:1, :]
+    across = column_sum((starts[0] + tops * early[...]) * late)
     across = per_head_sum(jnp.broadcast_to(across, (EDGE, width)), heads)[0:1, :]
     row, column = row_col()
     log_grad = (
@@ -450,7 +453,9 @@
     sums[1:2, for_heads] += column_sum(step_pre)
     step_out[...] = low(step_pre)
 
-    d_pre_x = (d_val + skip * d_mixed[...].astype(f32)) * slope_x
+    g = d_mixed[...].astype(f32)
+    sums[6:7, :width] += column_sum(g * (pre_x * sigma))
+    d_pre_x = (d_val + skip * g) * slope_x
     inner_x[EDGE:, :] = inx[...]
     of_x = slice(0, width)
     d_in = low(
@@ -471,16 +476,26 @@
     )
     bc_low[...] = low(d_in)
     shares = jnp.transpose(d_in)
-    share = bc_rows.shape[1]
+    share = bc_rows.shape[1] - 2 * EDGE
     for k in range(bc_rows.shape[0]):
-        bc_rows[k] = shares[k * share : (k + 1) * share, :]
+        bc_rows[k, :share, :] = shares[k * share : (k + 1) * share, :]
+        bc_rows[k, share:, :] = jnp.zeros((2 * EDGE, CHUNK), f32)
+
+    @pl.when(chunk == 0)
+    def _():
+        for row_at in range(5):
+            for j in range(2):
+                at = width + j * STATE
+                line = sums[row_at : row_at + 1, at : at + STATE]
+                to = share + 2 * row_at + j
+                for k in range(bc_rows.shape[0]):
+                    bc_rows[k, to : to + 1, :] = line
 
 
 def norm_back_kernel(
-    dg, dx, dbc, dst, ahead, hid, hid_block, gain, wz, wx, wbc, wdt, wout, sums, bc_rows, out, parts, scale, along, gains
+    buffer, dg, dx, dbc, dst, hid, gain, wz, wx, wbc, wdt, out, dots, scale, along
 ):
     i = pl.program_id(0)
-    last = pl.num_programs(0) - 1
     _, count, width = out.shape
 
     @pl.when(i == 0)
@@ -493,60 +508,55 @@
     total = dot_nt(dg[...], wz[...]) + dot_nt(dx[...], wx[...])
     total = total + dot_nt(dbc[...], wbc[...])
     total = total + dot(dst[:, : wdt.shape[0]], wdt[...])
-    out[0] = dot(ahead[...], wout[...])
-    out[1] = total
-    product = total * (hid_block[...].astype(f32) * scale[:, 0:1])
+    out[0] = total
     here = pl.ds(pl.multiple_of(i * width, width), width)
-    gains[0:1, here] = column_sum(product)
-    weighted = product * as_row(gain)
+    weighted = total * (hid[:, here].astype(f32) * scale[:, 0:1]) * as_row(gain)
     partial = weighted[:, :LANES]
     for k in range(1, width // LANES):
         partial = partial + weighted[:, k * LANES : (k + 1) * LANES]
     along[...] += partial
 
-    @pl.when(i == last)
+    @pl.when(i == pl.num_programs(0) - 1)
     def _():
-        heads, share = bc_rows.shape[0], bc_rows.shape[1]
-        first = dg.shape[1]
-        own = gains.shape[1] // heads
-        parts[...] = jnp.zeros(parts.shape, f32)
-        for k in range(heads):
-            parts[k, :share, :] = bc_rows[k]
-            parts[k, share : share + 5, : 2 * STATE] = sums[0:5, first : first + 2 * STATE]
-            parts[k, share + 5 : share + 6, :own] = gains[0:1, k * own : (k + 1) * own]
         for j in range(count // CHUNK):
             lanes = slice(j * CHUNK, (j + 1) * CHUNK)
             line = column_sum(jnp.transpose(along[lanes, :]))
-            for k in range(heads):
-                parts[k, share + 6 : share + 7, lanes] = line
-
-
-def share_kernel(buffer, parts, step_low, normed, sums, out, dots):
+            dots[:, lanes] = jnp.broadcast_to(line, (EDGE, CHUNK))
+
+
+def share_kernel(
+    buffer, parts, step_low, normed, sums, gains_z, gains_x, gain, wbc_rows, wdt, out
+):
     share = parts[0]
     for k in range(1, parts.shape[0]):
         share = share + parts[k]
-    count = share.shape[0] - EDGE
-    extra = share[count:, :]
-    dots[...] = extra
+    count = share.shape[0] - 2 * EDGE
+    extra = share[count:, :STATE]
     features = normed.shape[1]
-    own = features // parts.shape[0]
     width = features // 2
-    gains = jnp.concatenate([extra[5:6, :own], jnp.zeros((1, features - own), f32)], axis=1)
+    pairs = [
+        jnp.concatenate([extra[2 * r : 2 * r + 1, :], extra[2 * r + 1 : 2 * r + 2, :]], axis=1)
+        for r in range(EDGE)
+    ]
+    summed = jnp.concatenate(
+        [
+            jnp.zeros((EDGE, width), f32),
+            jnp.concatenate(pairs, axis=0),
+            jnp.zeros((EDGE, features - width - 2 * STATE), f32),
+        ],
+        axis=1,
+    )
+    steps = 2 * EDGE
+    of_w = dot(low(share[:count, :]), normed[...])
+    of_dt = dot_tn(step_low[...], normed[...])[:steps, :]
+    heads = wdt.shape[0]
+    gains = gains_z[0:1, :] + gains_x[0:1, :] + column_sum(of_w * wbc_rows[...].astype(f32))
+    gains = gains + column_sum(of_dt[:heads, :] * wdt[...].astype(f32))
+    gains = gains / as_row(gain)
     lane = lax.broadcasted_iota(jnp.int32, (EDGE, features), 1)
     row = lax.broadcasted_iota(jnp.int32, (EDGE, features), 0)
     of_bc = (lane >= width) & (lane < width + 2 * STATE) & (row < 5)
-    summed = jnp.concatenate(
-        [
-            jnp.zeros((EDGE, width), f32),
-            extra[:, : 2 * STATE],
-            jnp.zeros((EDGE, features - width - 2 * STATE), f32),
-        ],
-        axis=1,
-    )
     tiny = jnp.where(row == 7, gains, jnp.where(of_bc, summed, sums[...]))
-    steps = 2 * EDGE
-    of_w = dot(low(share[:count, :]), normed[...])
-    of_dt = dot_tn(step_low[...], normed[...])[:steps, :]
     ranges, rows, half = out.shape
     spare = jnp.zeros((rows * ranges * half // features - count - steps - EDGE, features), f32)
     stacked = jnp.concatenate([of_w, of_dt, tiny, spare], axis=0)
@@ -556,56 +566,70 @@
         out[k * per : (k + 1) * per] = stacked[:, k * half : (k + 1) * half].reshape(per, rows, half)
 
 
-def copy_kernel(source, out):
-    out[...] = source[...]
-
-
-def join_kernel(core, mine, theirs, out):
-    half = mine.shape[2]
-    per = mine.shape[0]
-    count = out.shape[0] // per
-    own = mine[:, :count, :].reshape(per * count, half)
-    other = theirs[:, :count, :].reshape(per * count, half)
-    out[:, :half] = jnp.where(core[0] == 0, own, other)
-    out[:, half:] = jnp.where(core[0] == 0, other, own)
+def place_kernel(core, blocks, out):
+    out[...] = blocks[:, : out.shape[0] // blocks.shape[0], :].reshape(out.shape)
 
 
 def deal_kernel(
-    mine, theirs, bc, dt, conv_x, conv_bc, bias_x, bias_bc, gain, norm_gain, by_head, sums
+    core, blocks, mine, theirs, onto,
+    out, bc, dt, conv_x, conv_bc, bias_x, bias_bc, gain, dt_bias, a_log, skip, sums,
 ):
-    share, steps = bc.shape[0], dt.shape[0]
-    taps, width = conv_x.shape
-    bc_width = conv_bc.shape[1]
-    total = mine[...] + theirs[...]
-    ranges, count, half = total.shape
-    blocks = bc.shape[1] // half
-    per = ranges // blocks
-    first = share + 2 * EDGE
-    for k in range(blocks):
-        lanes = slice(k * half, (k + 1) * half)
-        block = total[k * per : (k + 1) * per].reshape(per * count, half)
-        bc[:, lanes] = block[:share, :]
-        dt[:, lanes] = block[share : share + steps, :]
-        sums[:, lanes] = block[first : first + EDGE, :]
-    conv_x[...] = sums[:taps, :width]
-    bias_x[...] = sums[taps, :width]
-    conv_bc[...] = sums[:taps, width : width + bc_width]
-    bias_bc[...] = sums[taps, width : width + bc_width]
-    gain[...] = sums[5, :width]
-    norm_gain[...] = sums[7, : norm_gain.shape[0]]
-    by_head[...] = sums[:, width + bc_width : width + bc_width + LANES]
-    by_head[2:3, :] = per_head_sum(sums[:, :width], head_map(width))[6:7, :]
-
-
-def product_kernel(left, right, out):
-    out[...] = dot_tn(left[...], right[...])
-
-
-def outer_kernel(left, right, left_peer, right_peer, out):
-    product = dot_tn(left[...], right[...]) + dot_tn(low(left_peer[...]), low(right_peer[...]))
+    out[...] = blocks[:, : out.shape[0] // blocks.shape[0], :].reshape(out.shape)
+
+    @pl.when(pl.program_id(0) == 0)
+    def _():
+        share, steps = bc.shape[0], dt.shape[0]
+        taps, width = conv_x.shape
+        bc_width = conv_bc.shape[1]
+        total = mine[...] + theirs[...]
+        ranges, count, half = total.shape
+        per = ranges // (bc.shape[1] // half)
+        first = share + 2 * EDGE
+        for k in range(bc.shape[1] // half):
+            lanes = slice(k * half, (k + 1) * half)
+            block = total[k * per : (k + 1) * per].reshape(per * count, half)
+            bc[:, lanes] = block[:share, :]
+            dt[:, lanes] = block[share : share + steps, :]
+            sums[:, lanes] = block[first : first + EDGE, :]
+        conv_x[...] = sums[:taps, :width]
+        bias_x[...] = sums[taps, :width]
+        conv_bc[...] = sums[:taps, width : width + bc_width]
+        bias_bc[...] = sums[taps, width : width + bc_width]
+        gain[...] = sums[5, :width]
+        at = width + bc_width
+        a_log[...] = sums[0, at : at + steps]
+        dt_bias[...] = sums[1, at : at + steps]
+        skip[...] = per_head_sum(sums[:, :width], head_map(width))[6, :steps]
+
+
+def along_rows(value):
+    ones = jnp.ones((EDGE, value.shape[1]), bf16)
+    high, rest = parts_of(value, 2)
+    return dot_nt(ones, high) + dot_nt(ones, rest)
+
+
+def early_kernel(normed, gate_grad, w_z, normed_out, cot, z_out, out_out, gains):
+    product = dot_tn(normed[...], gate_grad[...])
+    z_out[...] = product
+    gains[...] = along_rows(product * w_z[...].astype(f32))
+    out_out[...] = dot_tn(normed_out[...], cot[...])
+
+
+def branch_kernel(left, right, out):
+    out[0] = dot(left[...], right[...])
+
+
+def round_kernel(source, out):
+    out[...] = low(source[...])
+
+
+def outer_kernel(core, left, right, left_peer, right_peer, weight, out, gains):
+    product = dot_tn(left[...], right[...]) + dot_tn(left_peer[...], low(right_peer[...]))
     per, _, half = out.shape
     count = product.shape[0] // per
     out[:, :count, :] = product.reshape(per, count, half)
+    lower, upper = weight[:, :half].astype(f32), weight[:, half:].astype(f32)
+    gains[...] = along_rows(product * jnp.where(core[0] == 0, lower, upper))
 
 
 def total_kernel(parts, out):
@@ -688,10 +712,11 @@
     def rows_back(columns):
         return pl.BlockSpec((CHUNK, columns), lambda i: (chunks - 1 - i, 0))
 
-    pair_line = pl.BlockSpec((parts_head, 2, CHUNK), lambda i: (0, 0, i))
+    pair_line = pl.BlockSpec((2, CHUNK), lambda i: (0, i))
     state_spec = pl.BlockSpec((1, STATE, width), lambda i: (i, 0, 0))
     state_back = pl.BlockSpec((1, STATE, width), lambda i: (chunks - 1 - i, 0, 0))
     dt_rows = w_dt.T
+    bc_own_rows = lax.dynamic_slice_in_dim(w_bc, head_pos * bc_share, bc_share, 1).T
     small = jnp.pad(
         jnp.stack([dt_bias, a_log, skip_d]), ((0, EDGE - 3), (0, LANES - heads_here))
     )
@@ -760,7 +785,17 @@
         blocks = array.reshape(ranges, parts, array.shape[1])
         return lax.all_to_all(blocks, "seq", 0, 0).reshape(array.shape)
 
-    received = exchanged(payload)
+    normed_peer = call(
+        round_kernel,
+        chunks,
+        [(normed_peer, rows(model_width))],
+        [((tokens, model_width), bf16, rows(model_width))],
+    )[0]
+    rows_all = hid.astype(f32)
+    scale_in = lax.rsqrt(jnp.mean(rows_all * rows_all, axis=1, keepdims=True) + epsilon)
+    received, normed_peer, bc_own_rows = lax.optimization_barrier(
+        (exchanged(payload), normed_peer, bc_own_rows)
+    )
     within = call(
         within_kernel,
         chunks,
@@ -770,6 +805,7 @@
             (step, rows(LANES)),
             (cumc, rows(LANES)),
             (starts, state_spec),
+            (small, small_spec),
         ],
         [((tokens, width), f32, rows(width))],
         flops=6 * tokens * CHUNK * width,
@@ -784,37 +820,37 @@
     )
     incoming = exchanged(incoming)
 
+    reads_rows = pl.BlockSpec((CHUNK, STATE), lambda i: (i, 1))
     mixed, sums = call(
         mix_kernel,
         chunks,
         [
             (incoming, whole((STATE, width))),
-            (pre_x, rows(width)),
-            (pre_bc, rows(bc_width)),
+            (pre_bc, reads_rows),
             (cumd, rows(LANES)),
             (within, rows(width)),
             (gate_z, rows(width)),
             (d_out, rows(width)),
-            (small, small_spec),
             (gain_out, whole((width,))),
         ],
-        [((tokens, width), f32, rows(width)), ((parts_head, 2, tokens), f32, pair_line)],
+        [((tokens, width), f32, rows(width)), ((2, tokens), f32, pair_line)],
         flops=2 * tokens * STATE * width,
         moved=10 << 20,
     )
-    totals = lax.all_to_all(sums, "head", 0, 0)
+    totals = [sums]
+    for by in range(1, parts_head):
+        pairs = [(i, (i + by) % parts_head) for i in range(parts_head)]
+        totals.append(lax.ppermute(sums, "head", pairs))
     normed_out, gate_low, d_mixed, col_out, payload = call(
         functools.partial(gate_kernel, width * parts_head),
         chunks,
         [
-            (totals, pair_line),
+            *[(line, pair_line) for line in totals],
             (mixed, rows(width)),
             (gate_z, rows(width)),
             (d_out, rows(width)),
-            (pre_x, rows(width)),
-            (pre_bc, rows(bc_width)),
+            (pre_bc, reads_rows),
             (cumd, rows(LANES)),
-            (small, small_spec),
             (gain_out, whole((width,))),
         ],
         [
@@ -830,7 +866,7 @@
 
     received = exchanged(payload)
     share = model_width // parts_head
-    d_values, d_bc, d_step, d_log, full_starts = call(
+    d_values, d_bc, d_step, d_log = call(
         back_kernel,
         chunks,
         [
@@ -848,24 +884,27 @@
             ((tokens, bc_width), f32, rows_back(bc_width)),
             ((tokens, LANES), f32, rows_back(LANES)),
             ((tokens, LANES), f32, rows_back(LANES)),
-            ((chunks, STATE, width), f32, state_back),
         ],
         [pltpu.VMEM((STATE, width), f32), pltpu.VMEM((LANES, CHUNK), f32)],
     )
     half_columns = pl.BlockSpec((tokens, half), lambda i: (0, i))
-    pair_columns = pl.BlockSpec((tokens, 2 * LANES), lambda i: (0, i))
-    grad_z = call(
-        product_kernel,
-        model_width // half,
-        [(normed, half_columns), (gate_low, whole((tokens, width)))],
-        [((model_width, width), f32, rows_of(half, width))],
-    )[0]
-    grad_out = call(
-        product_kernel,
-        width // (2 * LANES),
-        [(normed_out, pair_columns), (cot, whole((tokens, model_width)))],
-        [((width, model_width), f32, rows_of(2 * LANES, model_width))],
-    )[0]
+    gain_block = pl.BlockSpec((EDGE, half), lambda i: (0, i))
+    grad_z, grad_out, gains_z = call(
+        early_kernel,
+        model_width // (2 * LANES),
+        [
+            (normed, pl.BlockSpec((tokens, 2 * LANES), lambda i: (0, i))),
+            (gate_low, whole((tokens, width))),
+            (w_z, rows_of(2 * LANES, width)),
+            (normed_out, pl.BlockSpec((tokens, LANES), lambda i: (0, i))),
+            (cot, whole((tokens, model_width))),
+        ],
+        [
+            ((model_width, width), f32, rows_of(2 * LANES, width)),
+            ((width, model_width), f32, rows_of(LANES, model_width)),
+            ((EDGE, model_width), f32, pl.BlockSpec((EDGE, 2 * LANES), lambda i: (0, i))),
+        ],
+    )
     received, grad_z, grad_out = lax.optimization_barrier((received, grad_z, grad_out))
     grad_z, grad_out = lax.psum((grad_z, grad_out), ("dp", "seq"))
     later = call(
@@ -897,7 +936,22 @@
         ],
         [((EDGE, width + bc_width), f32, whole((EDGE, width + bc_width)))],
     )[0]
-    edge_next = from_behind(edge_grad, "seq", -1)
+    branch = call(
+        branch_kernel,
+        3,
+        [
+            (normed_out, whole((tokens, width))),
+            (w_out, pl.BlockSpec((width, 4 * LANES), lambda i: (0, i))),
+        ],
+        [
+            (
+                (2, tokens, model_width),
+                f32,
+                pl.BlockSpec((1, tokens, 4 * LANES), lambda i: (0, 0, i)),
+            )
+        ],
+    )[0]
+    edge_next, branch = lax.optimization_barrier((from_behind(edge_grad, "seq", -1), branch))
 
     def rows_before(columns):
         step_rows = CHUNK // EDGE
@@ -912,7 +966,8 @@
         [
             (core_flag, flag_spec),
             (later, whole((STATE, width))),
-            (full_starts, state_back),
+            (starts, state_back),
+            (incoming, whole((STATE, width))),
             (pre_x, rows_back(width)),
             (pre_bc, rows_back(bc_width)),
             (inner_x, rows_back(width)),
@@ -942,9 +997,11 @@
             ((tokens, half), f32, rows_back(half)),
             ((tokens, bc_width), bf16, rows_back(bc_width)),
             (
-                (parts_head, bc_share, tokens),
+                (parts_head, bc_share + 2 * EDGE, tokens),
                 f32,
-                pl.BlockSpec((parts_head, bc_share, CHUNK), lambda i: (0, 0, chunks - 1 - i)),
+                pl.BlockSpec(
+                    (parts_head, bc_share + 2 * EDGE, CHUNK), lambda i: (0, 0, chunks - 1 - i)
+                ),
             ),
             ((tokens, LANES), bf16, rows_back(LANES)),
             ((EDGE, model_width), f32, whole((EDGE, model_width))),
@@ -960,122 +1017,109 @@
     blocks = model_width // half
     per = ranges // blocks
     x_rows, small_rows = model_width // ranges, half // ranges
+    bc_parts = lax.all_to_all(bc_rows, "head", 0, 0)
+    shared = pl.BlockSpec((per, x_rows + small_rows, half), lambda i: (i, 0, 0))
+    small_block = pl.BlockSpec((ranges, small_rows, half), lambda i: (0, x_rows // small_rows, 0))
+    grad_x, gains_x = call(
+        outer_kernel,
+        blocks,
+        [
+            (core_flag, flag_spec),
+            (normed, half_columns),
+            (own, whole((tokens, half))),
+            (normed_peer, half_columns),
+            (peer, whole((tokens, half))),
+            (w_x, rows_of(half, width)),
+        ],
+        [
+            ((ranges, x_rows + small_rows, half), f32, shared),
+            ((EDGE, model_width), f32, gain_block),
+        ],
+    )
+    grad_x, bc_parts = lax.optimization_barrier((grad_x, bc_parts))
+    grad_x = call(
+        share_kernel,
+        1,
+        [
+            (grad_x, pl.BlockSpec(memory_space=pl.ANY)),
+            (bc_parts, whole(bc_parts.shape)),
+            (step_low, whole(step_low.shape)),
+            (normed, whole(normed.shape)),
+            (sums, whole(sums.shape)),
+            (gains_z, whole(gains_z.shape)),
+            (gains_x, whole(gains_x.shape)),
+            (norm_gain, whole((model_width,))),
+            (bc_own_rows, whole(bc_own_rows.shape)),
+            (dt_rows, whole(dt_rows.shape)),
+        ],
+        [(grad_x.shape, f32, small_block)],
+        aliases={0: 0},
+    )[0]
+
+    grad_x, x_low = lax.optimization_barrier((grad_x, x_low))
+    grad_x = lax.all_to_all(grad_x, "seq", 0, 0)
     features = 2 * LANES
-    feature_blocks = model_width // features
-    by_features = pl.BlockSpec((tokens, features), lambda i: (0, i))
-    both, parts_out = call(
+    both, dots = call(
         norm_back_kernel,
-        feature_blocks,
-        [
+        model_width // features,
+        [
+            (branch, pl.BlockSpec(memory_space=pl.ANY)),
             (gate_low, whole((tokens, width))),
             (x_low, whole((tokens, width))),
             (bc_low, whole((tokens, bc_width))),
             (step_low, whole((tokens, LANES))),
-            (normed_out, whole((tokens, width))),
             (hid, whole((tokens, model_width))),
-            (hid, by_features),
             (norm_gain, pl.BlockSpec((features,), lambda i: (i,))),
             (w_z, rows_of(features, width)),
             (w_x, rows_of(features, width)),
             (w_bc, rows_of(features, bc_width)),
             (dt_rows, pl.BlockSpec((heads_here, features), lambda i: (0, i))),
-            (w_out, pl.BlockSpec((width, features), lambda i: (0, i))),
-            (sums, whole((EDGE, model_width))),
-            (bc_rows, whole(bc_rows.shape)),
         ],
         [
             (
                 (2, tokens, model_width),
                 f32,
-                pl.BlockSpec((2, tokens, features), lambda i: (0, 0, i)),
+                pl.BlockSpec((1, tokens, features), lambda i: (1, 0, i)),
             ),
-            (
-                (parts_head, bc_share + EDGE, tokens),
-                f32,
-                whole((parts_head, bc_share + EDGE, tokens)),
-            ),
-        ],
-        [
-            pltpu.VMEM((tokens, LANES), f32),
-            pltpu.VMEM((tokens, LANES), f32),
-            pltpu.VMEM((EDGE, model_width), f32),
-        ],
-    )
-    bc_parts = lax.all_to_all(parts_out, "head", 0, 0)
-    shared = pl.BlockSpec((per, x_rows + small_rows, half), lambda i: (i, 0, 0))
-    small_block = pl.BlockSpec((ranges, small_rows, half), lambda i: (0, x_rows // small_rows, 0))
-    grad_x = call(
-        outer_kernel,
-        blocks,
-        [
-            (normed, half_columns),
-            (own, whole((tokens, half))),
-            (normed_peer, half_columns),
-            (peer, whole((tokens, half))),
-        ],
-        [((ranges, x_rows + small_rows, half), f32, shared)],
-    )[0]
-    grad_x, bc_parts = lax.optimization_barrier((grad_x, bc_parts))
-    grad_x, dots = call(
-        share_kernel,
-        1,
-        [
-            (grad_x, pl.BlockSpec(memory_space=pl.ANY)),
-            (bc_parts, whole(bc_parts.shape)),
-            (step_low, whole(step_low.shape)),
-            (normed, whole(normed.shape)),
-            (sums, whole(sums.shape)),
-        ],
-        [
-            (grad_x.shape, f32, small_block),
             ((EDGE, tokens), f32, whole((EDGE, tokens))),
         ],
+        [pltpu.VMEM((tokens, LANES), f32), pltpu.VMEM((tokens, LANES), f32)],
         aliases={0: 0},
     )
-    row_dot = dots[6]
-    branch_own, norm_own = lax.psum_scatter(both, "head", scatter_dimension=2, tiled=True)
-    grad_x = lax.all_to_all(grad_x, "seq", 0, 0)
+    grad_x, both, dots = lax.optimization_barrier((grad_x, both, dots))
     lane_block = pl.BlockSpec(grad_x.shape[:2] + (LANES,), lambda i: (0, 0, i))
     grad_x = call(
         total_kernel, half // LANES, [(grad_x, lane_block)], [(grad_x.shape, f32, lane_block)]
     )[0]
+    grad_x, both, dots = lax.optimization_barrier((grad_x, both, dots))
     grad_x = lax.all_to_all(grad_x, "seq", 0, 0)
-    grad_z = call(
-        copy_kernel,
-        blocks,
-        [(grad_z, rows_of(half, width))],
-        [((model_width, width), f32, rows_of(half, width))],
-    )[0]
-    grad_out = call(
-        copy_kernel,
-        blocks,
-        [(grad_out, rows_of(half // 2, model_width))],
-        [((width, model_width), f32, rows_of(half // 2, model_width))],
-    )[0]
-    branch_own, norm_own, grad_z, grad_out = lax.optimization_barrier(
-        (branch_own, norm_own, grad_z, grad_out)
-    )
-    first = head_pos * share
-    rows_own = lax.dynamic_slice_in_dim(hid, first, share, 1).astype(f32)
-    output = (rows_own + branch_own).astype(bf16)[None]
-    rows_all = hid.astype(f32)
-    scale_in = lax.rsqrt(jnp.mean(rows_all * rows_all, axis=1, keepdims=True) + epsilon)
-    gain_own = lax.dynamic_slice_in_dim(norm_gain, first, share, 0)
-    cot_own = lax.dynamic_slice_in_dim(cot, first, share, 1).astype(f32)
-    unit_own = rows_own * scale_in
-    grad_in = scale_in * (norm_own * gain_own - unit_own * row_dot[:, None] / model_width)
-    hidden_grad = (cot_own + grad_in).astype(bf16)[None]
-    grad_x, grad_z, grad_out, output, hidden_grad = lax.optimization_barrier(
-        (grad_x, grad_z, grad_out, output, hidden_grad)
-    )
+    reduced = lax.psum_scatter(both, "head", scatter_dimension=2, tiled=True)
+    row_dot = lax.psum(dots[0], "head")
+    grad_x, row_dot, scale_in = lax.optimization_barrier((grad_x, row_dot, scale_in))
     x_peer = swap_cores(grad_x)
     grads = grad_x
-    grad_x = call(
-        join_kernel,
-        blocks,
-        [(core_flag, flag_spec), (grads, shared), (x_peer, shared)],
-        [((model_width, width), f32, rows_of(half, width))],
-    )[0]
+    prefetched = functools.partial(
+        pl.pallas_call,
+        compiler_params=pltpu.CompilerParams(
+            dimension_semantics=("arbitrary",), vmem_limit_bytes=58 * 2**20
+        ),
+        cost_estimate=pl.CostEstimate(flops=0, bytes_accessed=0, transcendentals=0),
+    )
+    block = pl.BlockSpec((per, x_rows + small_rows, half), lambda i, core: (i, 0, 0))
+    half_of = pl.BlockSpec((half, half), lambda i, core: (i, core[0]))
+    full = jax.ShapeDtypeStruct((model_width, width), f32)
+    grad_x = prefetched(
+        place_kernel,
+        grid_spec=pltpu.PrefetchScalarGridSpec(
+            num_scalar_prefetch=1, grid=(blocks,), in_specs=[block], out_specs=half_of
+        ),
+        out_shape=full,
+    )(core_flag, grads)
+    tiny_at = bc_share + 2 * EDGE + 7
+    gains = grads.reshape(blocks, per, x_rows + small_rows, half)
+    gains = gains[:, tiny_at // small_rows, x_rows + tiny_at % small_rows, :]
+    gains = jnp.sum(lax.all_to_all(gains, "head", 0, 0), axis=0)
+    g_norm = gains + swap_cores(gains)
     taps = conv_x.shape[0]
     shapes = [
         (bc_share, model_width),
@@ -1085,20 +1129,42 @@
         (width,),
         (bc_width,),
         (width,),
-        (share,),
-        (EDGE, LANES),
+        (heads_here,),
+        (heads_here,),
+        (heads_here,),
     ]
-    dealt = call(
+
+    def fixed(shape):
+        return pl.BlockSpec(shape, lambda i, core: (0,) * len(shape))
+
+    tiny_block = pl.BlockSpec(
+        (ranges, small_rows, half), lambda i, core: (0, x_rows // small_rows, 0)
+    )
+    dealt = prefetched(
         deal_kernel,
-        1,
-        [
-            (grads, small_block),
-            (x_peer, small_block),
-        ],
-        [(shape, f32, whole(shape)) for shape in shapes],
-        [pltpu.VMEM((EDGE, model_width), f32)],
-    )
-    g_bc, g_dt, g_conv_x, g_conv_bc, g_bias_x, g_bias_bc, g_gain, g_norm, by_head = dealt
+        grid_spec=pltpu.PrefetchScalarGridSpec(
+            num_scalar_prefetch=1,
+            grid=(blocks,),
+            in_specs=[block, tiny_block, tiny_block, pl.BlockSpec(memory_space=pl.ANY)],
+            out_specs=[half_of] + [fixed(shape) for shape in shapes],
+            scratch_shapes=[pltpu.VMEM((EDGE, model_width), f32)],
+        ),
+        out_shape=[full] + [jax.ShapeDtypeStruct(shape, f32) for shape in shapes],
+        input_output_aliases={4: 0},
+    )(1 - core_flag, x_peer, grads, x_peer, grad_x)
+    grad_x, g_bc, g_dt, g_conv_x, g_conv_bc, g_bias_x, g_bias_bc, g_gain = dealt[:8]
+    g_dt_bias, g_a_log, g_skip = dealt[8:]
+    g_bc, grad_z, grad_out, g_norm = lax.optimization_barrier((g_bc, grad_z, grad_out, g_norm))
+    reduced, grad_z, grad_out = lax.optimization_barrier((reduced, grad_z, grad_out))
+    branch_own, norm_own = reduced[0], reduced[1]
+    first = head_pos * share
+    rows_own = lax.dynamic_slice_in_dim(hid, first, share, 1).astype(f32)
+    output = (rows_own + branch_own).astype(bf16)[None]
+    gain_own = lax.dynamic_slice_in_dim(norm_gain, first, share, 0)
+    cot_own = lax.dynamic_slice_in_dim(cot, first, share, 1).astype(f32)
+    unit_own = rows_own * scale_in
+    grad_in = scale_in * (norm_own * gain_own - unit_own * row_dot[:, None] / model_width)
+    hidden_grad = (cot_own + grad_in).astype(bf16)[None]
     return (
         output,
         hidden_grad,
@@ -1111,9 +1177,9 @@
         g_conv_bc,
         g_bias_x,
         g_bias_bc,
-        by_head[1, :heads_here],
-        by_head[0, :heads_here],
-        by_head[2, :heads_here],
+        g_dt_bias,
+        g_a_log,
+        g_skip,
         g_gain,
         grad_out,
     )

time: 314 us -> 312 us (level)
  blocking collectives: 57.3 us -> 14.7 us
  starting transfers between devices: 48.3 us -> 69.3 us
  waiting for transfers between devices: 56.6 us -> 67.7 us
  local copies, waits for them, and re-layouts: 9.4 us -> 17.8 us
    all_to_all x1 -> x2, waiting for transfers between devices: 0.01 us -> 61.8 us  [per_device(): grad_x = lax.all_to_all(grad_x, 'seq', 0, 0)]
    all_to_all x2 -> x1, blocking collectives: 57.3 us -> 6.78 us  [per_device(): gains = jnp.sum(lax.all_to_all(gains, 'head', 0, 0), axis=0)]
    psum x1, waiting for transfers between devices: 39.1 us -> 0.02 us  [per_device(): grad_z, grad_out = lax.psum((grad_z, grad_out), ('dp', 'seq'))]
    unnamed x24 -> x45, local copies, waits for them, and re-layouts: 5.1 us -> 16.1 us
    pallas_call x20 -> x17, Pallas kernels: 111 us -> 99.8 us  [call(): pl.pallas_call(kernel, grid=(grid,), in_specs=[spec for _, spec in ins],...]
    pallas_call x0 -> x2, Pallas kernels: none -> 8.82 us  [the longest x1 4.73 us: per_device(): prefetched(deal_kernel, grid_spec=pltpu.PrefetchScalarGridSpec(num_scalar...]
    psum x0 -> x1, blocking collectives: none -> 7.93 us  [per_device(): row_dot = lax.psum(dots[0], 'head')]
    ppermute x3 -> x4, waiting for transfers between devices: 7.85 us -> 0.01 us  [swap_cores(): return lax.ppermute(shard, 'dp', [(0, 1), (1, 0)])]
  transfers between devices with their start and end apart: 13 -> 18, of which waited for: 7 -> 6; matrix products, arithmetic and copies ran while one was open for 5% -> 5% of each run, Pallas kernels for 24% -> 29%
where the time goes in v2:
time: 312 us; the launch traced here: 309 us
  Pallas kernels  109 us (35%)
  starting transfers between devices  69.3 us (22%)
  waiting for transfers between devices  67.7 us (22%)
  local copies, waits for them, and re-layouts  17.8 us (6%)
  between operations  15.8 us (5%)
  blocking collectives  14.7 us (5%)
  matrix products  8.46 us (3%)
  other arithmetic  6.11 us (2%)
    pallas_call x17, Pallas kernels, call(): pl.pallas_call(kernel, grid=(grid,), in_specs=[spec for _, spec in ins],...  99.8 us
    all_to_all x2, waiting for transfers between devices, per_device(): grad_x = lax.all_to_all(grad_x, 'seq', 0, 0)  61.8 us
    all_to_all x4, starting transfers between devices, exchanged(): return lax.all_to_all(blocks, 'seq', 0, 0).reshape(array.shape)  27.7 us
    unnamed x45, local copies, waits for them, and re-layouts  16.1 us
    all_to_all x2, starting transfers between devices, per_device(): grad_x = lax.all_to_all(grad_x, 'seq', 0, 0)  14.3 us
    ppermute x4, starting transfers between devices, swap_cores(): return lax.ppermute(shard, 'dp', [(0, 1), (1, 0)])  13.6 us
    psum x1, blocking collectives, per_device(): row_dot = lax.psum(dots[0], 'head')  7.93 us
    all_to_all x1, blocking collectives, per_device(): gains = jnp.sum(lax.all_to_all(gains, 'head', 0, 0), axis=0)  6.78 us
  transfers between devices with their start and end apart: 18, of which 6 were waited for; matrix products, arithmetic and copies ran while one was open for 5% of the time, Pallas kernels for 29%

profile of v2, /device:TPU:1, one launch (start us, length us, event | category | flops | bytes accessed | tf_op | source)
XLA Modules:
  0.0 308.5 jit_solution(3317877457175945105)
XLA Ops:
  8.0 6.3 %shard_map.279 = (bf16[512,1536]{1,0:T(8,128)(2,1)}, f32[512,1536]{1,0:T(8,128)}, f32[512,768]{1,0:T(8,128)}, f32[512,256]{1,0:T(8,128)}, f32[512,128]{1,0:T(8,128)}, /*index=5*/f32[8,1024]{1,0:T(8,128)}) custom-call(bf16[512,1536]{1,0:T(8,128)(2,1)} %bitcast.31, f32[1536]{0:T(1024)} %gain.9, bf16[1536,768]{1,0:T(8,128)(2,1)} %wx.3, bf16[1536,256]{1,0:T(8,128)(2,1)} %wbc.3, ...), custom_call_target="tpu_custom_call" | custom-call | flops 1610612736 | bytes 18874368 | tf_op jit(solution)/shard_map/pallas_call | solution.py:647
  21.4 7.3 %shard_map.280 = (f32[512,768]{1,0:T(8,128)}, f32[512,256]{1,0:T(8,128)}, f32[512,128]{1,0:T(8,128)}, f32[512,128]{1,0:T(8,128)}, f32[512,128]{1,0:T(8,128)}, /*...) custom-call(f32[8,1024]{1,0:T(8,128)} %copy-done.11, f32[512,768]{1,0:T(8,128)} %get-tuple-element.97.inx.before_x, ...), custom_call_target="tpu_custom_call" | custom-call | flops 100663296 | bytes 8388608 | tf_op jit(solution)/shard_map/pallas_call | solution.py:647
  28.7 7.6 %all-to-all-start = ((f32[16,8,896]{2,1,0:T(8,128)}), f32[16,8,896]{2,1,0:T(8,128)S(1)}, u32[]{:S(2)}, u32[]{:S(2)}) async-start(f32[16,8,896]{2,1,0:T(8,128)} %bitcast.45), calls=%async_computation | async-start | bytes 917504 | tf_op jit(solution)/shard_map/all_to_all | solution.py:786
  48.5 6.7 %all-to-all-start.1 = ((f32[16,8,768]{2,1,0:T(8,128)}), f32[16,8,768]{2,1,0:T(8,128)S(1)}, u32[]{:S(2)}, u32[]{:S(2)}) async-start(f32[16,8,768]{2,1,0:T(8,128)} %bitcast.47), calls=%async_computation.1 | async-start | bytes 786432 | tf_op jit(solution)/shard_map/all_to_all | solution.py:786
  59.4 5.9 %shard_map.283.within = f32[512,768]{1,0:T(8,128)} custom-call(f32[512,768]{1,0:T(8,128)} %get-tuple-element.106.prex, f32[512,256]{1,0:T(8,128)} %get-tuple-element.104.prebc.pre_reads, f32[512,128]{1,0:T(8,128)} %get-tuple-element.107.step_in, f32[512,128]{1,0:T(8,128)} %get-tuple-element.108.cumc_in, f32[4,128,768]{2,1,0:T(8,128)} %get-tuple-element.109.starts, ...), custom_call_target="tpu_custom_call" | custom-call | flops 301989888 | bytes 8388608 | tf_op jit(solution)/shard_map/pallas_call | solution.py:647
  66.1 5.2 %shard_map.284 = (f32[512,768]{1,0:T(8,128)}, f32[2,512]{1,0:T(2,128)}) custom-call(f32[128,768]{1,0:T(8,128)} %bitcast.33, f32[512,256]{1,0:T(8,128)} %get-tuple-element.104.prebc.pre_reads, f32[512,128]{1,0:T(8,128)} %get-tuple-element.105.cumd.total.cumd_in, f32[512,768]{1,0:T(8,128)} %shard_map.283.within, f32[512,768]{1,0:T(8,128)} %fusion.9.gate_z, ...), custom_call_target="tpu_custom_call" | custom-call | flops 100663296 | bytes 10485760 | tf_op jit(solution)/shard_map/pallas_call | solution.py:647
  78.6 5.8 %shard_map.285 = (bf16[512,768]{1,0:T(8,128)(2,1)}, bf16[512,768]{1,0:T(8,128)(2,1)}, bf16[512,768]{1,0:T(8,128)(2,1)}, f32[8,768]{1,0:T(8,128)}, f32[128,768]{1,0:T(8,128)}) custom-call(f32[2,512]{1,0:T(2,128)} %get-tuple-element.110.totals, f32[2,512]{1,0:T(2,128)} %copy-done.13, f32[2,512]{1,0:T(2,128)} %copy-done.14, f32[2,512]{1,0:T(2,128)} %copy-done.15, ...), custom_call_target="tpu_custom_call" | custom-call | flops 100663296 | bytes 14680064 | tf_op jit(solution)/shard_map/pallas_call | solution.py:647
  84.4 6.8 %all-to-all-start.2 = ((f32[16,8,768]{2,1,0:T(8,128)}), f32[16,8,768]{2,1,0:T(8,128)S(1)}, u32[]{:S(2)}, u32[]{:S(2)}) async-start(f32[16,8,768]{2,1,0:T(8,128)} %bitcast.46), calls=%async_computation.2 | async-start | bytes 786432 | tf_op jit(solution)/shard_map/all_to_all | solution.py:786
  91.3 9.6 %shard_map.286 = (f32[1536,768]{1,0:T(8,128)}, f32[768,1536]{1,0:T(8,128)}, f32[8,1536]{1,0:T(8,128)}) custom-call(bf16[512,1536]{1,0:T(8,128)(2,1)} %get-tuple-element.95.normed.left, bf16[512,768]{1,0:T(8,128)(2,1)} %get-tuple-element.113.gate_grad.dg, bf16[1536,768]{1,0:T(8,128)(2,1)} %wz.1, bf16[512,768]{1,0:T(8,128)(2,1)} %get-tuple-element.114.normed_out.left, ...), custom_call_target="tpu_custom_call" | custom-call | tf_op jit(solution)/shard_map/pallas_call | solution.py:647
  103.5 6.7 %all-to-all-start.3 = ((f32[16,8,768]{2,1,0:T(8,128)}), f32[16,8,768]{2,1,0:T(8,128)S(1)}, u32[]{:S(2)}, u32[]{:S(2)}) async-start(f32[16,8,768]{2,1,0:T(8,128)} %bitcast.43), calls=%async_computation.3 | async-start | bytes 786432 | tf_op jit(solution)/shard_map/all_to_all | solution.py:786
  110.2 10.7 %shard_map.288 = (f32[512,768]{1,0:T(8,128)}, f32[512,256]{1,0:T(8,128)}, f32[512,128]{1,0:T(8,128)}, f32[512,128]{1,0:T(8,128)}) custom-call(f32[512,768]{1,0:T(8,128)} %get-tuple-element.106.prex, f32[512,256]{1,0:T(8,128)} %get-tuple-element.104.prebc.pre_reads, f32[512,128]{1,0:T(8,128)} %get-tuple-element.107.step_in, ...), custom_call_target="tpu_custom_call" | custom-call | tf_op jit(solution)/shard_map/pallas_call | solution.py:647
  125.2 5.3 %shard_map.290.buffer = f32[2,512,1536]{2,1,0:T(8,128)} custom-call(bf16[512,768]{1,0:T(8,128)(2,1)} %get-tuple-element.114.normed_out.left, bf16[768,1536]{1,0:T(8,128)(2,1)} %right.1), custom_call_target="tpu_custom_call" | custom-call | tf_op jit(solution)/shard_map/pallas_call | solution.py:647
  131.1 9.7 %shard_map.291 = (bf16[512,768]{1,0:T(8,128)(2,1)}, bf16[512,384]{1,0:T(8,128)(2,1)}, f32[512,384]{1,0:T(8,128)}, bf16[512,256]{1,0:T(8,128)(2,1)}, f32[4,80,512...) custom-call(s32[1]{0:T(128)} %bitcast.core, f32[128,768]{1,0:T(8,128)} %bitcast.39, ...), custom_call_target="tpu_custom_call" | custom-call | tf_op jit(solution)/shard_map/pallas_call | solution.py:647
  140.8 4.9 %collective-permute-start.6 = (f32[512,384]{1,0:T(8,128)}, f32[512,384]{1,0:T(8,128)S(1)}, u32[]{:S(2)}, u32[]{:S(2)}) collective-permute-start(f32[512,384]{1,0:T(8,128)} %get-tuple-element.128), channel_id=1, source_target_pairs={{0,64},{64,0},{1,65},{65,1},{2,66},{66,2},{3,67},{67,3},{4,68},{68... | collective-permute-start | bytes 2359304 | tf_op jit(solution)/shard_map/ppermute | solution.py:669
  150.2 6.4 %shard_map.292 = (f32[16,120,384]{2,1,0:T(8,128)}, f32[8,1536]{1,0:T(8,128)}) custom-call(s32[1]{0:T(128)} %bitcast.core, bf16[512,1536]{1,0:T(8,128)(2,1)} %get-tuple-element.95.normed.left, bf16[512,384]{1,0:T(8,128)(2,1)} %get-tuple-element.126.right, bf16[512,1536]{1,0:T(8,128)(2,1)} %shard_map.281.left_peer, f32[512,384]{1,0:T(8,128)} %copy-done.10, ...), custom_call_target="tpu_custom_call" | custom-call | tf_op jit(solution)/shard_map/pallas_call | solution.py:647
  164.2 8.3 %all-to-all-start.5 = ((f32[16,120,384]{2,1,0:T(8,128)}), f32[16,120,384]{2,1,0:T(8,128)S(1)}, u32[]{:S(2)}, u32[]{:S(2)}) async-start(f32[16,120,384]{2,1,0:T(8,128)} %shard_map.293), calls=%async_computation.5 | async-start | bytes 5898240 | tf_op jit(solution)/shard_map/all_to_all | solution.py:1060
  172.6 9.9 %shard_map.294 = (f32[2,512,1536]{2,1,0:T(8,128)}, f32[8,512]{1,0:T(8,128)}) custom-call(f32[2,512,1536]{2,1,0:T(8,128)} %shard_map.290.buffer, bf16[512,768]{1,0:T(8,128)(2,1)} %get-tuple-element.113.gate_grad.dg, bf16[512,768]{1,0:T(8,128)(2,1)} %get-tuple-element.141.dx, ...), custom_call_target="tpu_custom_call", output_to_operand_aliasing={{0}: (0, {})} | custom-call | tf_op jit(solution)/shard_map/pallas_call | solution.py:647
  182.5 29.8 %all-to-all-done.5.parts = f32[16,120,384]{2,1,0:T(8,128)S(1)} async-done(((f32[16,120,384]{2,1,0:T(8,128)}), f32[16,120,384]{2,1,0:T(8,128)S(1)}, u32[]{:S(2)}, u32[]{:S(2)}) %all-to-all-start.5) | async-done | bytes 2949152 | tf_op jit(solution)/shard_map/all_to_all | solution.py:1060
  218.4 5.9 %all-to-all-start.6 = ((f32[16,120,384]{2,1,0:T(8,128)}), f32[16,120,384]{2,1,0:T(8,128)S(1)}, u32[]{:S(2)}, u32[]{:S(2)}) async-start(f32[16,120,384]{2,1,0:T(8,128)} %shard_map.295), calls=%async_computation.7 | async-start | bytes 5898240 | tf_op jit(solution)/shard_map/all_to_all | solution.py:1095
  226.9 7.9 %psum.21 = f32[512]{0:T(512)S(1)} all-reduce(f32[512]{0:T(512)S(1)} %bitcast.51), channel_id=1, replica_groups=mesh['dp'=2,'seq'=16,'head'=4] {'head'}, use_global_device_ids=true, to_apply=%region_1.2 | all-reduce | flops 512 | bytes 4096 | tf_op jit(solution)/shard_map/psum | solution.py:1097
  234.9 31.9 %all-to-all-done.6.blocks.mine = f32[16,120,384]{2,1,0:T(8,128)S(1)} async-done(((f32[16,120,384]{2,1,0:T(8,128)}), f32[16,120,384]{2,1,0:T(8,128)S(1)}, u32[]{:S(2)}, u32[]{:S(2)}) %all-to-all-start.6) | async-done | bytes 2949152 | tf_op jit(solution)/shard_map/all_to_all | solution.py:1095
  266.8 6.0 %collective-permute-start.7 = (f32[16,120,384]{2,1,0:T(8,128)S(1)}, f32[16,120,384]{2,1,0:T(8,128)}, u32[]{:S(2)}, u32[]{:S(2)}) collective-permute-start(f32[16,120,384]{2,1,0:T(8,128)S(1)} %all-to-all-done.6.blocks.mine), channel_id=1, source_target_pairs={{0,64},{64,0},{1,65},{65,1},{2,66},{66,2},{3,67},{67,3},{4,68},{68... | collective-permute-start | bytes 8847368 | tf_op jit(solution)/shard_map/ppermute | solution.py:669
  272.8 6.8 %all_to_all.44 = f32[4,1,384]{2,1,0:T(1,128)S(1)} all-to-all(f32[4,1,384]{2,1,0:T(1,128)S(1)} %slice_bitcast_fusion), channel_id=1, replica_groups=mesh['dp'=2,'seq'=16,'head'=4] {'head'}, dimensions={0} | all-to-all | bytes 12288 | tf_op jit(solution)/shard_map/all_to_all | solution.py:1121
  294.0 4.9 %copy.43 = f32[1536,768]{1,0:T(8,128)} copy(f32[1536,768]{1,0:T(8,128)} %get-tuple-element.181) | data formatting | bytes 9437184
  (93 shorter events, 76.5 us)
Async XLA Ops:
  8.0 11.4 %copy-start.16 = (f32[12]{0:T(128)S(1)}, f32[12]{0:T(128)}, u32[]{:S(2)}) copy-start(f32[12]{0:T(128)} %param.29) | copy-start | bytes 148
  8.0 11.4 %copy-start.17 = (f32[12]{0:T(128)S(1)}, f32[12]{0:T(128)}, u32[]{:S(2)}) copy-start(f32[12]{0:T(128)} %param.28) | copy-start | bytes 148
  14.3 22.0 %copy-start.8 = (bf16[1536,256]{1,0:T(8,128)(2,1)S(1)}, bf16[1536,256]{1,0:T(8,128)(2,1)}, u32[]{:S(2)}) copy-start(bf16[1536,256]{1,0:T(8,128)(2,1)} %wbc.3) | copy-start | bytes 2359300
  14.3 27.2 %collective-permute-start.1 = (f32[512,1536]{1,0:T(8,128)}, f32[512,1536]{1,0:T(8,128)}, u32[]{:S(2)}, u32[]{:S(2)}) collective-permute-start(f32[512,1536]{1,0:T(8,128)} %get-tuple-element.101), channel_id=1, source_target_pairs={{0,64},{64,0},{1,65},{65,1},{2,66},{66,2},{3,67},{67,3},{4,68},{68... | collective-permute-start | bytes 9437192 | tf_op jit(solution)/shard_map/ppermute | solution.py:669
  15.8 4.9 %collective-permute-start = (f32[8,1024]{1,0:T(8,128)}, f32[8,1024]{1,0:T(8,128)S(1)}, u32[]{:S(2)}, u32[]{:S(2)}) collective-permute-start(f32[8,1024]{1,0:T(8,128)} %get-tuple-element.96), channel_id=1, source_target_pairs={{0,4},{4,8},{8,12},{12,16},{16,20},{20,24},{24,28},{28,32},{32,36}... | collective-permute-start | bytes 98312 | tf_op jit(solution)/shard_map/ppermute | solution.py:665
  21.4 16.0 %copy-start.1 = (bf16[512,1536]{1,0:T(8,128)(2,1)S(1)}, bf16[512,1536]{1,0:T(8,128)(2,1)}, u32[]{:S(2)}) copy-start(bf16[512,1536]{1,0:T(8,128)(2,1)} %get-tuple-element.95.normed.left) | copy-start | bytes 4718596
  28.7 16.9 %all-to-all-start = ((f32[16,8,896]{2,1,0:T(8,128)}), f32[16,8,896]{2,1,0:T(8,128)S(1)}, u32[]{:S(2)}, u32[]{:S(2)}) async-start(f32[16,8,896]{2,1,0:T(8,128)} %bitcast.45), calls=%async_computation | async-start | bytes 917504 | tf_op jit(solution)/shard_map/all_to_all | solution.py:786
  41.6 13.6 %copy-start.6 = (bf16[1,512,1536]{2,1,0:T(8,128)(2,1)S(1)}, bf16[1,512,1536]{2,1,0:T(8,128)(2,1)}, u32[]{:S(2)}) copy-start(bf16[1,512,1536]{2,1,0:T(8,128)(2,1)} %param.17) | copy-start | bytes 4718596
  48.5 16.8 %all-to-all-start.1 = ((f32[16,8,768]{2,1,0:T(8,128)}), f32[16,8,768]{2,1,0:T(8,128)S(1)}, u32[]{:S(2)}, u32[]{:S(2)}) async-start(f32[16,8,768]{2,1,0:T(8,128)} %bitcast.47), calls=%async_computation.1 | async-start | bytes 786432 | tf_op jit(solution)/shard_map/all_to_all | solution.py:786
  71.3 5.0 %collective-permute-start.2 = (f32[2,512]{1,0:T(2,128)}, f32[2,512]{1,0:T(2,128)S(1)}, u32[]{:S(2)}, u32[]{:S(2)}) collective-permute-start(f32[2,512]{1,0:T(2,128)} %get-tuple-element.110.totals), channel_id=1, source_target_pairs={{0,1},{1,2},{2,3},{3,0},{4,5},{5,6},{6,7},{7,4},{8,9},{9,10},{10,1... | collective-permute-start | bytes 12296 | tf_op jit(solution)/shard_map/ppermute | solution.py:843
  72.6 4.2 %collective-permute-start.3 = (f32[2,512]{1,0:T(2,128)}, f32[2,512]{1,0:T(2,128)S(1)}, u32[]{:S(2)}, u32[]{:S(2)}) collective-permute-start(f32[2,512]{1,0:T(2,128)} %get-tuple-element.110.totals), channel_id=1, source_target_pairs={{0,2},{1,3},{2,0},{3,1},{4,6},{5,7},{6,4},{7,5},{8,10},{9,11},{10,... | collective-permute-start | bytes 12296 | tf_op jit(solution)/shard_map/ppermute | solution.py:843
  75.2 2.8 collective-permute-start.4
  84.4 16.5 %all-to-all-start.2 = ((f32[16,8,768]{2,1,0:T(8,128)}), f32[16,8,768]{2,1,0:T(8,128)S(1)}, u32[]{:S(2)}, u32[]{:S(2)}) async-start(f32[16,8,768]{2,1,0:T(8,128)} %bitcast.46), calls=%async_computation.2 | async-start | bytes 786432 | tf_op jit(solution)/shard_map/all_to_all | solution.py:786
  91.2 199.8 %all-reduce.4.cloned.1.call-start = ((), (), s32[]{:S(2)}) async-start(), calls=%async_computation.10 | async-start | bytes 18874368 | tf_op jit(solution)/shard_map/psum | solution.py:909
  103.5 17.4 %all-to-all-start.3 = ((f32[16,8,768]{2,1,0:T(8,128)}), f32[16,8,768]{2,1,0:T(8,128)S(1)}, u32[]{:S(2)}, u32[]{:S(2)}) async-start(f32[16,8,768]{2,1,0:T(8,128)} %bitcast.43), calls=%async_computation.3 | async-start | bytes 786432 | tf_op jit(solution)/shard_map/all_to_all | solution.py:786
  123.7 6.8 %collective-permute-start.5 = (f32[8,1024]{1,0:T(8,128)}, f32[8,1024]{1,0:T(8,128)S(1)}, u32[]{:S(2)}, u32[]{:S(2)}) collective-permute-start(f32[8,1024]{1,0:T(8,128)} %shard_map.289), channel_id=1, source_target_pairs={{4,0},{8,4},{12,8},{16,12},{20,16},{24,20},{28,24},{32,28},{36,32}... | collective-permute-start | bytes 98312 | tf_op jit(solution)/shard_map/ppermute | solution.py:665
  140.8 8.5 %collective-permute-start.6 = (f32[512,384]{1,0:T(8,128)}, f32[512,384]{1,0:T(8,128)S(1)}, u32[]{:S(2)}, u32[]{:S(2)}) collective-permute-start(f32[512,384]{1,0:T(8,128)} %get-tuple-element.128), channel_id=1, source_target_pairs={{0,64},{64,0},{1,65},{65,1},{2,66},{66,2},{3,67},{67,3},{4,68},{68... | collective-permute-start | bytes 2359304 | tf_op jit(solution)/shard_map/ppermute | solution.py:669
  145.7 14.3 %all-to-all-start.4 = ((f32[4,80,512]{2,1,0:T(8,128)}), f32[4,80,512]{2,1,0:T(8,128)S(1)}, u32[]{:S(2)}, u32[]{:S(2)}) async-start(f32[4,80,512]{2,1,0:T(8,128)} %get-tuple-element.130), calls=%async_computation.4 | async-start | bytes 1310720 | tf_op jit(solution)/shard_map/all_to_all | solution.py:1020
  164.2 48.1 %all-to-all-start.5 = ((f32[16,120,384]{2,1,0:T(8,128)}), f32[16,120,384]{2,1,0:T(8,128)S(1)}, u32[]{:S(2)}, u32[]{:S(2)}) async-start(f32[16,120,384]{2,1,0:T(8,128)} %shard_map.293), calls=%async_computation.5 | async-start | bytes 5898240 | tf_op jit(solution)/shard_map/all_to_all | solution.py:1060
  172.6 118.4 %reduce-scatter.2.cloned.1.call-start = ((), (), s32[]{:S(2)}) async-start(), calls=%async_computation.9 | async-start | bytes 7864320 | tf_op jit(solution)/shard_map/reduce_scatter | solution.py:1096
  218.4 48.4 %all-to-all-start.6 = ((f32[16,120,384]{2,1,0:T(8,128)}), f32[16,120,384]{2,1,0:T(8,128)S(1)}, u32[]{:S(2)}, u32[]{:S(2)}) async-start(f32[16,120,384]{2,1,0:T(8,128)} %shard_map.295), calls=%async_computation.7 | async-start | bytes 5898240 | tf_op jit(solution)/shard_map/all_to_all | solution.py:1095
  266.8 14.8 %copy-start = (f32[16,120,384]{2,1,0:T(8,128)}, f32[16,120,384]{2,1,0:T(8,128)S(1)}, u32[]{:S(2)}) copy-start(f32[16,120,384]{2,1,0:T(8,128)S(1)} %all-to-all-done.6.blocks.mine) | copy-start | bytes 8847364
  266.8 19.4 %collective-permute-start.7 = (f32[16,120,384]{2,1,0:T(8,128)S(1)}, f32[16,120,384]{2,1,0:T(8,128)}, u32[]{:S(2)}, u32[]{:S(2)}) collective-permute-start(f32[16,120,384]{2,1,0:T(8,128)S(1)} %all-to-all-done.6.blocks.mine), channel_id=1, source_target_pairs={{0,64},{64,0},{1,65},{65,1},{2,66},{66,2},{3,67},{67,3},{4,68},{68... | collective-permute-start | bytes 8847368 | tf_op jit(solution)/shard_map/ppermute | solution.py:669
  279.6 6.1 %collective-permute-start.8 = (f32[384]{0:T(512)S(1)}, f32[384]{0:T(512)S(1)}, u32[]{:S(2)}, u32[]{:S(2)}) collective-permute-start(f32[384]{0:T(512)S(1)} %reduce_sum.19), channel_id=1, source_target_pairs={{0,64},{64,0},{1,65},{65,1},{2,66},{66,2},{3,67},{67,3},{4,68},{68... | collective-permute-start | bytes 4616 | tf_op jit(solution)/shard_map/ppermute | solution.py:669
  (15 other events, 35.4 us)
Sparse Core Ops, SparseCore 0:
  101.1 184.9 all-reduce.3
Sparse Core Ops, SparseCore 1:
  218.4 65.7 reduce-scatter.1
